TPU v7x, 32 devices: a whole 2x2x4 slice. The times are simulated.
32 devices in a mesh: dp: 8 (over z, x), mp: 4 (over y, core).
Axes of the slice: x: 2, y: 2, z: 4, core: 2. Of those that a mesh axis runs over, the one named last changes fastest.
Arguments:
- encoder_input: bfloat16 [12288, 512], P(('dp', 'mp')), may hold values from -6 to 6
- decoder_copy: bfloat16 [12288, 512], P(('dp', 'mp')), may hold values from -6 to 6
- decoder_target: bfloat16 [12288, 512], P(('dp', 'mp')), may hold values from -6 to 6
- decoder_cotangent: bfloat16 [12288, 512], P(('dp', 'mp')), may hold values from -6 to 6
- source_segments: int32 [8, 1536], P('dp'), may hold values from 0 to 23, never falling along the last dimension, each value on 1 to 128 neighbouring positions
- target_segments: int32 [8, 1536], P('dp'), may hold values from 0 to 23, never falling along the last dimension, each value on 1 to 128 neighbouring positions
- glance_mask: int32 [8, 1536], P('dp', 'mp'), may hold values 0 or 1
- attention_in: float32 [9, 512, 512], P(None, 'dp', 'mp')
- attention_out: float32 [3, 512, 512], P(None, 'mp', 'dp')
- feed_in: float32 [2, 512, 2048], P(None, 'dp', 'mp')
- feed_out: float32 [2, 2048, 512], P(None, 'mp', 'dp')
- norm_params: float32 [5, 2, 512], P(None, None, 'dp')
- attention_in_first: float32 [9, 512, 512], P(None, 'dp', 'mp')
- attention_out_first: float32 [3, 512, 512], P(None, 'mp', 'dp')
- feed_in_first: float32 [2, 512, 2048], P(None, 'dp', 'mp')
- feed_out_first: float32 [2, 2048, 512], P(None, 'mp', 'dp')
- norm_params_first: float32 [5, 2, 512], P(None, None, 'dp')
- attention_in_second: float32 [9, 512, 512], P(None, 'dp', 'mp'), as said below
- attention_out_second: float32 [3, 512, 512], P(None, 'mp', 'dp'), as said below
- feed_in_second: float32 [2, 512, 2048], P(None, 'dp', 'mp'), as said below
- feed_out_second: float32 [2, 2048, 512], P(None, 'mp', 'dp'), as said below
- norm_params_second: float32 [5, 2, 512], P(None, None, 'dp'), as said below
Outputs:
- encoder_output: bfloat16 [12288, 512], P(('dp', 'mp'))
- decoder_output: bfloat16 [12288, 512], P(('dp', 'mp'))
- encoder_input_grad: float32 [12288, 512], P(('dp', 'mp'))
- decoder_input_grad: float32 [12288, 512], P(('dp', 'mp'))
- grad_norm: float32 [], replicated
- attention_in_new: float32 [9, 512, 512], P(None, 'dp', 'mp')
- attention_out_new: float32 [3, 512, 512], P(None, 'mp', 'dp')
- feed_in_new: float32 [2, 512, 2048], P(None, 'dp', 'mp')
- feed_out_new: float32 [2, 2048, 512], P(None, 'mp', 'dp')
- norm_params_new: float32 [5, 2, 512], P(None, None, 'dp')
- attention_in_first_new: float32 [9, 512, 512], P(None, 'dp', 'mp')
- attention_out_first_new: float32 [3, 512, 512], P(None, 'mp', 'dp')
- feed_in_first_new: float32 [2, 512, 2048], P(None, 'dp', 'mp')
- feed_out_first_new: float32 [2, 2048, 512], P(None, 'mp', 'dp')
- norm_params_first_new: float32 [5, 2, 512], P(None, None, 'dp')
- attention_in_second_new: float32 [9, 512, 512], P(None, 'dp', 'mp')
- attention_out_second_new: float32 [3, 512, 512], P(None, 'mp', 'dp')
- feed_in_second_new: float32 [2, 512, 2048], P(None, 'dp', 'mp')
- feed_out_second_new: float32 [2, 2048, 512], P(None, 'mp', 'dp')
- norm_params_second_new: float32 [5, 2, 512], P(None, None, 'dp')
Inputs may be any that keep to these rules, and one draw needn't show every extreme that they name: `source_segments`: in each row segment numbers start at 0, never fall and end at 23; every sentence has 1 to 128 positions. `target_segments`: in each row segment numbers start at 0, never fall and end at 23; every sentence has 1 to 128 positions. `attention_in_second`: positive. `attention_out_second`: positive. `feed_in_second`: positive. `feed_out_second`: positive. `norm_params_second`: positive.
All inputs are finite; a program needn't handle non-finite values. No bound on the sum of `glance_mask` on one device may be relied on, other than what follows from the above.
Results may differ from a plain program's by a relative error of at most 0.03.
The roundings to bfloat16 on the way count: a program that leaves them out, or rounds other values in their place, can miss the bound.
Values may be sent and summed in bfloat16 or wider, within the bound.
No kernel may reach another device: no remote copies, remote signals or barrier semaphores. Data moves between devices by JAX's collectives and lax.ppermute only.
A program may use at most 192 MiB of HBM per device.

v0:
```python
import jax
import jax.numpy as jnp
from jax import lax
from jax.sharding import PartitionSpec as P

HEAD_DIM = 64
STEP = 10


norm_eps = 1e-05
beta_one = 0.9
beta_two = 0.98
adam_eps = 1e-08
weight_decay = 0.01
rate_matrix = 0.1
rate_norm = 0.5
clip_bound = 1.0
masked_score = -1e30


def layer_norm(totals, norm_gain, norm_shift):
    centred = totals - jnp.mean(totals, axis=-1, keepdims=True)
    spread = jnp.mean(centred * centred, axis=-1, keepdims=True)
    return centred * lax.rsqrt(spread + norm_eps) * norm_gain + norm_shift


def norm_back(totals, norm_gain, norm_shift, grad_out):
    outputs, pullback = jax.vjp(layer_norm, totals, norm_gain, norm_shift)
    return pullback(grad_out)


def gather_rows(values):
    return lax.all_gather(values, "mp", axis=0, tiled=True)


def sum_rows(row_term, row_count):
    return lax.psum_scatter(
        row_term(jnp.int32(0), row_count * lax.axis_size("mp")),
        "mp",
        scatter_dimension=0,
        tiled=True,
    )


def forward_term(operand, weights):
    return jnp.dot(operand, weights, preferred_element_type=jnp.float32)


def forward_branch(operand, weights_local):
    return lax.psum_scatter(
        forward_term(operand, weights_local), "mp", scatter_dimension=0, tiled=True
    )


def backward_term(factor_pairs):

    def row_term(offset, length):
        summed = None
        for operand, weights in factor_pairs:
            product = jnp.einsum("tc,dc->td", operand, weights, preferred_element_type=jnp.float32)
            summed = product if summed is None else summed + product
        return summed

    return row_term


def split_heads(matrix):
    return matrix.reshape(matrix.shape[0], matrix.shape[1] // HEAD_DIM, HEAD_DIM)


def project_three(rows_low, weights):
    return jnp.einsum("td,kdc->ktc", rows_low, weights, preferred_element_type=jnp.float32).astype(
        jnp.bfloat16
    )


def attend_forward(queries, keys_all, values_all, query_segments, key_segments):
    length_all, heads_local = (queries.shape[0], queries.shape[1])
    block_size = min(512, length_all)
    blocks = length_all // block_size
    query_blocks = queries.reshape(blocks, block_size, heads_local, HEAD_DIM)
    segment_blocks = query_segments.reshape(blocks, block_size)
    score_scale = HEAD_DIM ** (-0.5)

    def one_block(inputs_block):
        query_part, segment_part = inputs_block
        scores = (
            jnp.einsum("bhd,khd->hbk", query_part, keys_all, preferred_element_type=jnp.float32)
            * score_scale
        )
        allowed = segment_part[:, None] == key_segments[None, :]
        scores = jnp.where(allowed[None], scores, masked_score)
        highest = jnp.max(scores, axis=-1, keepdims=True)
        raised = jnp.exp(scores - highest)
        sums_exp = jnp.sum(raised, axis=-1, keepdims=True)
        attention_probs = (raised / sums_exp).astype(jnp.bfloat16)
        context = jnp.einsum(
            "hbk,khd->bhd", attention_probs, values_all, preferred_element_type=jnp.float32
        )
        return (context.astype(jnp.bfloat16), (highest + jnp.log(sums_exp))[..., 0])

    context, log_sums = lax.map(one_block, (query_blocks, segment_blocks))
    return (context.reshape(length_all, heads_local * HEAD_DIM), log_sums)


def attend_backward(
    queries, keys_all, values_all, query_segments, key_segments, log_sums, context_grad
):
    length_all, heads_local = (queries.shape[0], queries.shape[1])
    block_size = min(512, length_all)
    blocks = length_all // block_size
    query_blocks = queries.reshape(blocks, block_size, heads_local, HEAD_DIM)
    segment_blocks = query_segments.reshape(blocks, block_size)
    grad_blocks = context_grad.reshape(blocks, block_size, heads_local, HEAD_DIM)
    score_scale = HEAD_DIM ** (-0.5)

    def one_block(carried, inputs_block):
        key_grad, value_grad = carried
        query_part, segment_part, log_part, grad_part = inputs_block
        scores = (
            jnp.einsum("bhd,khd->hbk", query_part, keys_all, preferred_element_type=jnp.float32)
            * score_scale
        )
        allowed = segment_part[:, None] == key_segments[None, :]
        scores = jnp.where(allowed[None], scores, masked_score)
        attention_probs = jnp.exp(scores - log_part[..., None])
        value_grad = value_grad + jnp.einsum(
            "hbk,bhd->khd",
            attention_probs.astype(jnp.bfloat16),
            grad_part,
            preferred_element_type=jnp.float32,
        )
        prob_grad = jnp.einsum(
            "bhd,khd->hbk", grad_part, values_all, preferred_element_type=jnp.float32
        )
        centre = jnp.sum(attention_probs * prob_grad, axis=-1, keepdims=True)
        score_grad = (attention_probs * (prob_grad - centre)).astype(jnp.bfloat16)
        query_grad = (
            jnp.einsum("hbk,khd->bhd", score_grad, keys_all, preferred_element_type=jnp.float32)
            * score_scale
        )
        key_grad = key_grad + jnp.einsum(
            "hbk,bhd->khd", score_grad, query_part, preferred_element_type=jnp.float32
        )
        return ((key_grad, value_grad), query_grad.astype(jnp.bfloat16))

    empty_grad = jnp.zeros(keys_all.shape, jnp.float32)
    (key_grad, value_grad), query_grad = lax.scan(
        one_block, (empty_grad, empty_grad), (query_blocks, segment_blocks, log_sums, grad_blocks)
    )
    length_keys = keys_all.shape[0]
    width_local = heads_local * HEAD_DIM
    query_grad = query_grad.reshape(length_all, width_local)
    key_grad = (key_grad * score_scale).astype(jnp.bfloat16).reshape(length_keys, width_local)
    value_grad = value_grad.astype(jnp.bfloat16).reshape(length_keys, width_local)
    return (query_grad, key_grad, value_grad)


def attention_core(query_projected, key_projected, value_projected, query_segments, key_segments):
    queries = split_heads(query_projected)
    keys_all = split_heads(key_projected)
    values_all = split_heads(value_projected)
    context, log_sums = attend_forward(queries, keys_all, values_all, query_segments, key_segments)
    return (queries, keys_all, values_all, context, log_sums)


def attention_back(
    saved, query_inputs, key_inputs, query_segments, key_segments, weights_out, branch_grad
):
    queries, keys_all, values_all, context, log_sums = saved
    grad_gathered = gather_rows(branch_grad.astype(jnp.bfloat16))
    context_grad = jnp.einsum(
        "td,cd->tc", grad_gathered, weights_out, preferred_element_type=jnp.float32
    ).astype(jnp.bfloat16)
    out_grad = jnp.einsum("tc,td->cd", context, grad_gathered, preferred_element_type=jnp.float32)
    query_grad, key_grad, value_grad = attend_backward(
        queries, keys_all, values_all, query_segments, key_segments, log_sums, context_grad
    )
    in_grads = jnp.stack(
        [
            jnp.einsum("td,tc->dc", query_inputs, query_grad, preferred_element_type=jnp.float32),
            jnp.einsum("td,tc->dc", key_inputs, key_grad, preferred_element_type=jnp.float32),
            jnp.einsum("td,tc->dc", key_inputs, value_grad, preferred_element_type=jnp.float32),
        ]
    )
    return ((query_grad, key_grad, value_grad), in_grads, out_grad)


def feed_back(
    inputs_gathered,
    pre_values,
    hidden_values,
    weights_first,
    weights_second,
    branch_grad,
    row_count,
):
    grad_gathered = gather_rows(branch_grad.astype(jnp.bfloat16))
    hidden_grad = jnp.einsum(
        "td,fd->tf", grad_gathered, weights_second, preferred_element_type=jnp.float32
    )
    pre_grad = jax.vjp(jax.nn.gelu, pre_values)[1](hidden_grad)[0].astype(jnp.bfloat16)
    first_grad = jnp.einsum(
        "td,tf->df", inputs_gathered, pre_grad, preferred_element_type=jnp.float32
    )
    second_grad = jnp.einsum(
        "tf,td->fd", hidden_values, grad_gathered, preferred_element_type=jnp.float32
    )
    input_grad = sum_rows(backward_term(((pre_grad, weights_first),)), row_count)
    return (input_grad, first_grad, second_grad)


def adam_step(weights, first, second, grads, rate, decay):
    first_new = beta_one * first + (1.0 - beta_one) * grads
    second_new = beta_two * second + (1.0 - beta_two) * grads * grads
    first_hat = first_new / (1.0 - beta_one**STEP)
    second_hat = second_new / (1.0 - beta_two**STEP)
    weights_new = weights - rate * (first_hat / (jnp.sqrt(second_hat) + adam_eps) + decay * weights)
    return (weights_new, first_new, second_new)


def on_device(
    encoder_input,
    decoder_copy,
    decoder_target,
    decoder_cotangent,
    source_segments,
    target_segments,
    glance_mask,
    attention_in,
    attention_out,
    feed_in,
    feed_out,
    norm_params,
    attention_in_first,
    attention_out_first,
    feed_in_first,
    feed_out_first,
    norm_params_first,
    attention_in_second,
    attention_out_second,
    feed_in_second,
    feed_out_second,
    norm_params_second,
):
    row_count = encoder_input.shape[0]
    masters = (attention_in, attention_out, feed_in, feed_out, norm_params)
    lowered = [weights.astype(jnp.bfloat16) for weights in masters]
    gathered_in, gathered_out, gathered_first, gathered_second, gathered_norms = (
        lax.all_gather(lowered[0], "dp", axis=1, tiled=True),
        lax.all_gather(lowered[1], "dp", axis=2, tiled=True),
        lax.all_gather(lowered[2], "dp", axis=1, tiled=True),
        lax.all_gather(lowered[3], "dp", axis=2, tiled=True),
        lax.all_gather(lowered[4], "dp", axis=2, tiled=True),
    )
    norm_values = gathered_norms.astype(jnp.float32)
    source_row = source_segments[0]
    target_row = target_segments[0]
    encoder_gathered = gather_rows(encoder_input)
    projected = project_three(encoder_gathered, gathered_in[0:3])
    encoder_saved = attention_core(projected[0], projected[1], projected[2], source_row, source_row)
    branch = forward_branch(encoder_saved[3], gathered_out[0])
    first_total = encoder_input.astype(jnp.float32) + branch
    first_norm = layer_norm(first_total, norm_values[0, 0], norm_values[0, 1])
    first_gathered = gather_rows(first_norm.astype(jnp.bfloat16))
    first_pre = jnp.dot(first_gathered, gathered_first[0], preferred_element_type=jnp.float32)
    first_hidden = jax.nn.gelu(first_pre).astype(jnp.bfloat16)
    branch = forward_branch(first_hidden, gathered_second[0])
    second_total = first_norm + branch
    second_norm = layer_norm(second_total, norm_values[1, 0], norm_values[1, 1])
    encoder_output = second_norm.astype(jnp.bfloat16)
    picked = glance_mask[0] == 1
    decoder_input = jnp.where(picked[:, None], decoder_target, decoder_copy)
    decoder_gathered = gather_rows(decoder_input)
    projected = project_three(decoder_gathered, gathered_in[3:6])
    decoder_saved = attention_core(projected[0], projected[1], projected[2], target_row, target_row)
    branch = forward_branch(decoder_saved[3], gathered_out[1])
    third_total = decoder_input.astype(jnp.float32) + branch
    third_norm = layer_norm(third_total, norm_values[2, 0], norm_values[2, 1])
    query_gathered = gather_rows(third_norm.astype(jnp.bfloat16))
    memory_gathered = gather_rows(encoder_output)
    query_projected = jnp.dot(
        query_gathered, gathered_in[6], preferred_element_type=jnp.float32
    ).astype(jnp.bfloat16)
    memory_projected = project_three(memory_gathered, gathered_in[7:9])
    cross_saved = attention_core(
        query_projected, memory_projected[0], memory_projected[1], target_row, source_row
    )
    branch = forward_branch(cross_saved[3], gathered_out[2])
    fourth_total = third_norm + branch
    fourth_norm = layer_norm(fourth_total, norm_values[3, 0], norm_values[3, 1])
    fourth_gathered = gather_rows(fourth_norm.astype(jnp.bfloat16))
    second_pre = jnp.dot(fourth_gathered, gathered_first[1], preferred_element_type=jnp.float32)
    second_hidden = jax.nn.gelu(second_pre).astype(jnp.bfloat16)
    branch = forward_branch(second_hidden, gathered_second[1])
    fifth_total = fourth_norm + branch
    fifth_norm = layer_norm(fifth_total, norm_values[4, 0], norm_values[4, 1])
    decoder_output = fifth_norm.astype(jnp.bfloat16)
    gathered_in, gathered_out, gathered_first, gathered_second, gathered_norms = (
        lax.all_gather(lowered[0], "dp", axis=1, tiled=True),
        lax.all_gather(lowered[1], "dp", axis=2, tiled=True),
        lax.all_gather(lowered[2], "dp", axis=1, tiled=True),
        lax.all_gather(lowered[3], "dp", axis=2, tiled=True),
        lax.all_gather(lowered[4], "dp", axis=2, tiled=True),
    )
    norm_values = gathered_norms.astype(jnp.float32)
    fifth_grad, gain_four, shift_four = norm_back(
        fifth_total, norm_values[4, 0], norm_values[4, 1], decoder_cotangent.astype(jnp.float32)
    )
    input_grad, first_four, second_four = feed_back(
        fourth_gathered,
        second_pre,
        second_hidden,
        gathered_first[1],
        gathered_second[1],
        fifth_grad,
        row_count,
    )
    fourth_grad, gain_three, shift_three = norm_back(
        fourth_total, norm_values[3, 0], norm_values[3, 1], fifth_grad + input_grad
    )
    cross_grads, cross_in, cross_out = attention_back(
        cross_saved,
        query_gathered,
        memory_gathered,
        target_row,
        source_row,
        gathered_out[2],
        fourth_grad,
    )
    query_input_grad = sum_rows(backward_term(((cross_grads[0], gathered_in[6]),)), row_count)
    memory_grad = sum_rows(
        backward_term(((cross_grads[1], gathered_in[7]), (cross_grads[2], gathered_in[8]))),
        row_count,
    )
    third_grad, gain_two, shift_two = norm_back(
        third_total, norm_values[2, 0], norm_values[2, 1], fourth_grad + query_input_grad
    )
    self_grads, self_in, self_out = attention_back(
        decoder_saved,
        decoder_gathered,
        decoder_gathered,
        target_row,
        target_row,
        gathered_out[1],
        third_grad,
    )
    decoder_back = sum_rows(
        backward_term(
            (
                (self_grads[0], gathered_in[3]),
                (self_grads[1], gathered_in[4]),
                (self_grads[2], gathered_in[5]),
            )
        ),
        row_count,
    )
    decoder_input_grad = third_grad + decoder_back
    second_grad, gain_one, shift_one = norm_back(
        second_total, norm_values[1, 0], norm_values[1, 1], memory_grad
    )
    input_grad, first_zero, second_zero = feed_back(
        first_gathered,
        first_pre,
        first_hidden,
        gathered_first[0],
        gathered_second[0],
        second_grad,
        row_count,
    )
    first_grad, gain_zero, shift_zero = norm_back(
        first_total, norm_values[0, 0], norm_values[0, 1], second_grad + input_grad
    )
    encoder_grads, encoder_in, encoder_out = attention_back(
        encoder_saved,
        encoder_gathered,
        encoder_gathered,
        source_row,
        source_row,
        gathered_out[0],
        first_grad,
    )
    encoder_back = sum_rows(
        backward_term(
            (
                (encoder_grads[0], gathered_in[0]),
                (encoder_grads[1], gathered_in[1]),
                (encoder_grads[2], gathered_in[2]),
            )
        ),
        row_count,
    )
    encoder_input_grad = first_grad + encoder_back
    grad_in = jnp.concatenate([encoder_in, self_in, cross_in], axis=0)
    grad_out = jnp.stack([encoder_out, self_out, cross_out])
    grad_first = jnp.stack([first_zero, first_four])
    grad_second = jnp.stack([second_zero, second_four])
    grad_norms = jnp.stack(
        [
            jnp.stack([gain_zero, shift_zero]),
            jnp.stack([gain_one, shift_one]),
            jnp.stack([gain_two, shift_two]),
            jnp.stack([gain_three, shift_three]),
            jnp.stack([gain_four, shift_four]),
        ]
    )
    grad_norms = lax.psum(grad_norms, "mp")
    reduced = (
        lax.psum_scatter(grad_in, "dp", scatter_dimension=1, tiled=True),
        lax.psum_scatter(grad_out, "dp", scatter_dimension=2, tiled=True),
        lax.psum_scatter(grad_first, "dp", scatter_dimension=1, tiled=True),
        lax.psum_scatter(grad_second, "dp", scatter_dimension=2, tiled=True),
        lax.psum_scatter(grad_norms, "dp", scatter_dimension=2, tiled=True),
    )
    squares = jnp.sum(reduced[0] * reduced[0]) + jnp.sum(reduced[1] * reduced[1])
    squares = squares + jnp.sum(reduced[2] * reduced[2]) + jnp.sum(reduced[3] * reduced[3])
    squares = squares + jnp.sum(reduced[4] * reduced[4]) / lax.axis_size("mp")
    grad_norm = jnp.sqrt(lax.psum(squares, ("dp", "mp")))
    factor = clip_bound / jnp.maximum(grad_norm, clip_bound)
    firsts = (
        attention_in_first,
        attention_out_first,
        feed_in_first,
        feed_out_first,
        norm_params_first,
    )
    seconds = (
        attention_in_second,
        attention_out_second,
        feed_in_second,
        feed_out_second,
        norm_params_second,
    )
    results = []
    for number in range(5):
        rate = rate_norm if number == 4 else rate_matrix
        decay = 0.0 if number == 4 else weight_decay
        results.append(
            adam_step(
                masters[number],
                firsts[number],
                seconds[number],
                reduced[number] * factor,
                rate,
                decay,
            )
        )
    return (
        encoder_output,
        decoder_output,
        encoder_input_grad,
        decoder_input_grad,
        grad_norm,
        results[0][0],
        results[1][0],
        results[2][0],
        results[3][0],
        results[4][0],
        results[0][1],
        results[1][1],
        results[2][1],
        results[3][1],
        results[4][1],
        results[0][2],
        results[1][2],
        results[2][2],
        results[3][2],
        results[4][2],
    )


def solution(mesh):
    placed = (
        P(("dp", "mp"), None),
        P(("dp", "mp"), None),
        P(("dp", "mp"), None),
        P(("dp", "mp"), None),
        P("dp", None),
        P("dp", None),
        P("dp", "mp"),
        P(None, "dp", "mp"),
        P(None, "mp", "dp"),
        P(None, "dp", "mp"),
        P(None, "mp", "dp"),
        P(None, None, "dp"),
        P(None, "dp", "mp"),
        P(None, "mp", "dp"),
        P(None, "dp", "mp"),
        P(None, "mp", "dp"),
        P(None, None, "dp"),
        P(None, "dp", "mp"),
        P(None, "mp", "dp"),
        P(None, "dp", "mp"),
        P(None, "mp", "dp"),
        P(None, None, "dp"),
    )
    return jax.shard_map(
        on_device,
        mesh=mesh,
        in_specs=placed,
        out_specs=(
            P(("dp", "mp"), None),
            P(("dp", "mp"), None),
            P(("dp", "mp"), None),
            P(("dp", "mp"), None),
            P(),
            P(None, "dp", "mp"),
            P(None, "mp", "dp"),
            P(None, "dp", "mp"),
            P(None, "mp", "dp"),
            P(None, None, "dp"),
            P(None, "dp", "mp"),
            P(None, "mp", "dp"),
            P(None, "dp", "mp"),
            P(None, "mp", "dp"),
            P(None, None, "dp"),
            P(None, "dp", "mp"),
            P(None, "mp", "dp"),
            P(None, "dp", "mp"),
            P(None, "mp", "dp"),
            P(None, None, "dp"),
        ),
        check_vma=False,
    )
```

profile of v0, /device:TPU:0, one launch (start us, length us, event | category | flops | bytes accessed | tf_op | source)
XLA Modules:
  0.0 1333.0 jit_solution(7401595472454401115)
XLA Ops:
  11.3 33.1 %all_gather.55 = bf16[3,128,512]{1,2,0:T(8,128)(2,1)S(1)} all-gather(bf16[3,128,64]{1,2,0:T(8,128)(2,1)S(1)} %convert_element_type.185), channel_id=1, replica_groups=mesh['dp'=8,'mp'=4] {'dp'}, dimensions={2}, use_global_device_ids=true | all-gather | bytes 442368 | tf_op jit(solution)/shard_map/all_gather | solution.py:251
  44.5 10.8 all-gather.15.cloned.1.call-done
  55.3 20.2 %all-gather.17.cloned.1.call-done = bf16[1536,512]{1,0:T(8,128)(2,1)} async-done(((bf16[384,512]{1,0:T(8,128)(2,1)}), bf16[1536,512]{1,0:T(8,128)(2,1)}) %all-gather.17.cloned.1.call-update) | async-done | bytes 1572880 | tf_op jit(solution)/shard_map/all_gather | solution.py:33
  79.8 24.2 %while.81 = (s32[]{:T(128)}, bf16[3,512,2,64]{1,3,2,0:T(8,128)(2,1)S(1)}, f32[3,2,512]{2,1,0:T(2,128)S(1)}, s32[3,512]{1,0:T(4,128)S(1)}, s32[1,1536]{1,0:T(1,12...) while((s32[]{:T(128)}, ...), condition=%wide.region_3.4_spmd, body=%wide.region_0.3_spmd.sunk | while | flops 422378496 | bytes 23126144 | solution.py:102
  108.8 31.0 %all_gather.56 = bf16[5,2,512]{0,1,2:T(2,128)(2,1)S(1)} all-gather(bf16[5,2,64]{0,1,2:T(2,128)(2,1)S(1)} %copy.235), channel_id=1, replica_groups=mesh['dp'=8,'mp'=4] {'dp'}, dimensions={2}, use_global_device_ids=true | all-gather | bytes 11520 | tf_op jit(solution)/shard_map/all_gather | solution.py:254
  140.0 18.2 %slice_reduce_fusion.1 = (f32[512]{0:T(512)}, f32[512]{0:T(512)}, f32[512]{0:T(512)}, f32[512]{0:T(512)}, f32[512]{0:T(512)S(1)}, /*index=5*/f32[512]{0:T(512)S(...) fusion(f32[5,2,512]{0,1,2:T(2,128)S(1)} %convert_element_type.187), kind=kLoop, calls=%fused_computation.278 | loop fusion | bytes 40960 | tf_op jit(solution)/shard_map/slice | solution.py:297
  171.0 24.2 %while.82 = (s32[]{:T(128)}, bf16[3,512,2,64]{1,3,2,0:T(8,128)(2,1)S(1)}, f32[3,2,512]{2,1,0:T(2,128)S(1)}, s32[3,512]{1,0:T(4,128)S(1)}, s32[1,1536]{1,0:T(1,12...) while((s32[]{:T(128)}, ...), condition=%wide.region_13.14_spmd, body=%wide.region_10.13_spmd.sunk | while | flops 422378496 | bytes 23126144 | solution.py:102
  198.0 11.7 all-gather.21.cloned.1.call-done
  209.8 20.5 %all-gather.19.cloned.1.call-done = bf16[1536,512]{1,0:T(8,128)(2,1)} async-done(((bf16[384,512]{1,0:T(8,128)(2,1)}), bf16[1536,512]{1,0:T(8,128)(2,1)}) %all-gather.19.cloned.1.call-update) | async-done | bytes 1572880 | tf_op jit(solution)/shard_map/all_gather | solution.py:33
  234.4 39.1 %all-gather.23.cloned.1.call-done = bf16[2,512,512]{1,2,0:T(8,128)(2,1)} async-done(((bf16[2,512,64]{1,2,0:T(8,128)(2,1)}), bf16[2,512,512]{1,2,0:T(8,128)(2,1)}) %all-gather.23.cloned.1.call-update) | async-done | bytes 1048592 | tf_op jit(solution)/shard_map/all_gather | solution.py:253
  278.4 34.5 %reduce-scatter.21.cloned.1.call-done = f32[384,512]{1,0:T(8,128)} async-done(((f32[1536,512]{1,0:T(8,128)}), f32[384,512]{1,0:T(8,128)}) %reduce-scatter.21.cloned.1.call-update) | async-done | bytes 786448 | tf_op jit(solution)/shard_map/reduce_scatter | solution.py:50
  315.5 37.9 %reduce-scatter.19.cloned.1.call-done = f32[384,512]{1,0:T(8,128)} async-done(((f32[1536,512]{1,0:T(8,128)}), f32[384,512]{1,0:T(8,128)}) %reduce-scatter.19.cloned.1.call-update) | async-done | bytes 786448 | tf_op jit(solution)/shard_map/reduce_scatter | solution.py:50
  357.6 17.6 %all-gather.27.cloned.1.call-done = bf16[1536,512]{1,0:T(8,128)(2,1)} async-done(((bf16[384,512]{1,0:T(8,128)(2,1)}), bf16[1536,512]{1,0:T(8,128)(2,1)}) %all-gather.27.cloned.1.call-update) | async-done | bytes 1572880 | tf_op jit(solution)/shard_map/all_gather | solution.py:33
  379.2 17.9 %all-gather.29.cloned.1.call-done = bf16[1536,512]{1,0:T(8,128)(2,1)} async-done(((bf16[384,512]{1,0:T(8,128)(2,1)}), bf16[1536,512]{1,0:T(8,128)(2,1)}) %all-gather.29.cloned.1.call-update) | async-done | bytes 1572880 | tf_op jit(solution)/shard_map/all_gather | solution.py:33
  400.1 24.2 %while.83 = (s32[]{:T(128)}, bf16[3,512,2,64]{1,3,2,0:T(8,128)(2,1)S(1)}, f32[3,2,512]{2,1,0:T(2,128)S(1)}, s32[3,512]{1,0:T(4,128)S(1)}, s32[1,1536]{1,0:T(1,12...) while((s32[]{:T(128)}, ...), condition=%wide.region_20.21_spmd, body=%wide.region_17.20_spmd.sunk | while | flops 422378496 | bytes 23126144 | solution.py:102
  427.8 38.0 %reduce-scatter.23.cloned.1.call-done = f32[384,512]{1,0:T(8,128)} async-done(((f32[1536,512]{1,0:T(8,128)}), f32[384,512]{1,0:T(8,128)}) %reduce-scatter.23.cloned.1.call-update) | async-done | bytes 786448 | tf_op jit(solution)/shard_map/reduce_scatter | solution.py:50
  468.6 19.8 %all-gather.31.cloned.1.call-done = bf16[1536,512]{1,0:T(8,128)(2,1)} async-done(((bf16[384,512]{1,0:T(8,128)(2,1)}), bf16[1536,512]{1,0:T(8,128)(2,1)}) %all-gather.31.cloned.1.call-update) | async-done | bytes 1572880 | tf_op jit(solution)/shard_map/all_gather | solution.py:33
  495.5 38.0 %reduce-scatter.25.cloned.1.call-done = f32[384,512]{1,0:T(8,128)} async-done(((f32[1536,512]{1,0:T(8,128)}), f32[384,512]{1,0:T(8,128)}) %reduce-scatter.25.cloned.1.call-update) | async-done | bytes 786448 | tf_op jit(solution)/shard_map/reduce_scatter | solution.py:50
  538.4 19.6 %all-gather.33.cloned.1.call-done = bf16[1536,512]{1,0:T(8,128)(2,1)} async-done(((bf16[384,512]{1,0:T(8,128)(2,1)}), bf16[1536,512]{1,0:T(8,128)(2,1)}) %all-gather.33.cloned.1.call-update) | async-done | bytes 1572880 | tf_op jit(solution)/shard_map/all_gather | solution.py:33
  568.7 38.1 %reduce-scatter.27.cloned.1.call-done = f32[384,512]{1,0:T(8,128)} async-done(((f32[1536,512]{1,0:T(8,128)}), f32[384,512]{1,0:T(8,128)}) %reduce-scatter.27.cloned.1.call-update) | async-done | bytes 786448 | tf_op jit(solution)/shard_map/reduce_scatter | solution.py:37
  611.2 19.8 %all-gather.35.cloned.1.call-done = bf16[1536,512]{1,0:T(8,128)(2,1)} async-done(((bf16[384,512]{1,0:T(8,128)(2,1)}), bf16[1536,512]{1,0:T(8,128)(2,1)}) %all-gather.35.cloned.1.call-update) | async-done | bytes 1572880 | tf_op jit(solution)/shard_map/all_gather | solution.py:33
  635.7 38.9 %while.84 = (s32[]{:T(128)}, f32[1536,2,64]{0,2,1:T(8,128)}, f32[1536,2,64]{0,2,1:T(8,128)S(1)}, bf16[3,512,2,64]{1,3,2,0:T(8,128)(2,1)}, bf16[3,512,2,64]{1,3,2...) while((s32[]{:T(128)}, f32[1536,2,64]{0,2,1:T(8,128)}, ...), condition=%wide.region_34.35_spmd.clone, body=%wide.region_32.34_spmd.clone.sunk | while | flops 1022491648 | bytes 53784748 | solution.py:148
  685.6 33.0 %reduce-scatter.29.cloned.1.call-done = f32[384,512]{1,0:T(8,128)} async-done(((f32[1536,512]{1,0:T(8,128)}), f32[384,512]{1,0:T(8,128)}) %reduce-scatter.29.cloned.1.call-update) | async-done | bytes 786448 | tf_op jit(solution)/shard_map/reduce_scatter | solution.py:37
  718.6 40.7 %reduce-scatter.35.cloned.1.call-done = f32[384,512]{1,0:T(8,128)} async-done(((f32[1536,512]{1,0:T(8,128)}), f32[384,512]{1,0:T(8,128)}) %reduce-scatter.35.cloned.1.call-update) | async-done | bytes 786448 | tf_op jit(solution)/shard_map/reduce_scatter | solution.py:37
  763.6 19.8 %all-gather.37.cloned.1.call-done = bf16[1536,512]{1,0:T(8,128)(2,1)} async-done(((bf16[384,512]{1,0:T(8,128)(2,1)}), bf16[1536,512]{1,0:T(8,128)(2,1)}) %all-gather.37.cloned.1.call-update) | async-done | bytes 1572880 | tf_op jit(solution)/shard_map/all_gather | solution.py:33
  795.6 34.9 %reduce-scatter.31.cloned.1.call-done = f32[384,512]{1,0:T(8,128)} async-done(((f32[1536,512]{1,0:T(8,128)}), f32[384,512]{1,0:T(8,128)}) %reduce-scatter.31.cloned.1.call-update) | async-done | bytes 786448 | tf_op jit(solution)/shard_map/reduce_scatter | solution.py:37
  865.9 41.0 %while.86 = (s32[]{:T(128)}, f32[1536,2,64]{0,2,1:T(8,128)}, f32[1536,2,64]{0,2,1:T(8,128)S(1)}, bf16[3,512,2,64]{1,3,2,0:T(8,128)(2,1)}, bf16[3,512,2,64]{1,3,2...) while((s32[]{:T(128)}, f32[1536,2,64]{0,2,1:T(8,128)}, ...), condition=%wide.region_50.51_spmd.clone, body=%wide.region_48.50_spmd.clone.sunk | while | flops 1022491648 | bytes 53784748 | solution.py:148
  932.3 40.0 %while.85 = (s32[]{:T(128)}, f32[1536,2,64]{0,2,1:T(8,128)S(1)}, f32[1536,2,64]{0,2,1:T(8,128)S(1)}, bf16[3,512,2,64]{1,3,2,0:T(8,128)(2,1)}, bf16[3,512,2,64]{1...) while((s32[]{:T(128)}, f32[1536,2,64]{0,2,1:T(8,128)S(1)}, ...), condition=%wide.region_43.44_spmd.clone, body=%wide.region_41.43_spmd.clone.sunk | while | flops 1022491648 | bytes 53784748 | solution.py:148
  1017.5 124.5 %all-reduce.5.cloned.1.call-done = (f32[3,128,512]{1,0,2:T(4,128)}, f32[2,512,512]{1,0,2:T(2,128)}) async-done(((f32[3,128,512]{1,0,2:T(4,128)}, f32[2,512,512]{1,0,2:T(2,128)}), (f32[3,128,512]{1,0,2:T(4,128)}, f32[2,512,512]{1,0,2:T(2,128)})) %all-reduce.5.cloned.1.call-update) | async-done | bytes 2883600
  1145.5 86.9 %reduce-scatter.39.cloned.1.call-done = f32[9,64,128]{2,0,1:T(8,128)} async-done(((f32[9,512,128]{2,0,1:T(8,128)}), f32[9,64,128]{2,0,1:T(8,128)}) %reduce-scatter.39.cloned.1.call-update) | async-done | bytes 294928 | tf_op jit(solution)/shard_map/reduce_scatter | solution.py:409
  1236.9 36.0 %reduce-scatter.37.cloned.1.call-done = f32[384,512]{1,0:T(8,128)} async-done(((f32[1536,512]{1,0:T(8,128)}), f32[384,512]{1,0:T(8,128)}) %reduce-scatter.37.cloned.1.call-update) | async-done | bytes 786448 | tf_op jit(solution)/shard_map/reduce_scatter | solution.py:37
  1275.0 39.4 %psum.15 = f32[]{:T(128)} all-reduce(f32[]{:T(128)S(6)} %add.414), channel_id=1, replica_groups=mesh['dp'=8,'mp'=4] {'dp','mp'}, use_global_device_ids=true, to_apply=%region_73.74 | all-reduce | flops 1 | bytes 8 | tf_op jit(solution)/shard_map/psum | solution.py:418
  (635 shorter events, 429.3 us)
Async XLA Ops:
  7.2 48.1 %all-gather.15.cloned.1.call-start = ((), (), s32[]{:S(2)}) async-start(), calls=%async_computation.14 | async-start | bytes 1327104 | tf_op jit(solution)/shard_map/all_gather | solution.py:250
  8.9 66.5 %all-gather.17.cloned.1.call-start = ((), (), s32[]{:S(2)}) async-start(), calls=%async_computation.15 | async-start | bytes 1966080 | tf_op jit(solution)/shard_map/all_gather | solution.py:33
  9.7 148.5 %reduce-scatter.17.cloned.1.call-start = ((), (), s32[]{:S(2)}) async-start(), calls=%async_computation.16 | async-start | bytes 3932160 | tf_op jit(solution)/shard_map/reduce_scatter | solution.py:50
  44.5 380.2 %copy-start.29 = (bf16[3,128,512]{1,2,0:T(8,128)(2,1)}, bf16[3,128,512]{1,2,0:T(8,128)(2,1)S(1)}, u32[]{:S(2)}) copy-start(bf16[3,128,512]{1,2,0:T(8,128)(2,1)S(1)} %all_gather.55) | copy-start | bytes 1179652
  106.8 59.8 %all-gather.25.cloned.1.call-start = ((), (), s32[]{:S(2)}) async-start(), calls=%async_computation.21 | async-start | bytes 1966080 | tf_op jit(solution)/shard_map/all_gather | solution.py:33
  107.8 101.9 %all-gather.21.cloned.1.call-start = ((), (), s32[]{:S(2)}) async-start(), calls=%async_computation.18 | async-start | bytes 1179648 | tf_op jit(solution)/shard_map/all_gather | solution.py:252
  108.6 121.7 %all-gather.19.cloned.1.call-start = ((), (), s32[]{:S(2)}) async-start(), calls=%async_computation.17 | async-start | bytes 1966080 | tf_op jit(solution)/shard_map/all_gather | solution.py:33
  160.8 112.7 %all-gather.23.cloned.1.call-start = ((), (), s32[]{:S(2)}) async-start(), calls=%async_computation.19 | async-start | bytes 1179648 | tf_op jit(solution)/shard_map/all_gather | solution.py:253
  161.6 151.4 %reduce-scatter.21.cloned.1.call-start = ((), (), s32[]{:S(2)}) async-start(), calls=%async_computation.22 | async-start | bytes 3932160 | tf_op jit(solution)/shard_map/reduce_scatter | solution.py:50
  198.0 155.5 %reduce-scatter.19.cloned.1.call-start = ((), (), s32[]{:S(2)}) async-start(), calls=%async_computation.20 | async-start | bytes 3932160 | tf_op jit(solution)/shard_map/reduce_scatter | solution.py:50
  278.4 96.8 %all-gather.27.cloned.1.call-start = ((), (), s32[]{:S(2)}) async-start(), calls=%async_computation.23 | async-start | bytes 1966080 | tf_op jit(solution)/shard_map/all_gather | solution.py:33
  315.5 81.7 %all-gather.29.cloned.1.call-start = ((), (), s32[]{:S(2)}) async-start(), calls=%async_computation.24 | async-start | bytes 1966080 | tf_op jit(solution)/shard_map/all_gather | solution.py:33
  356.2 109.6 %reduce-scatter.23.cloned.1.call-start = ((), (), s32[]{:S(2)}) async-start(), calls=%async_computation.25 | async-start | bytes 3932160 | tf_op jit(solution)/shard_map/reduce_scatter | solution.py:50
  427.7 60.6 %all-gather.31.cloned.1.call-start = ((), (), s32[]{:S(2)}) async-start(), calls=%async_computation.26 | async-start | bytes 1966080 | tf_op jit(solution)/shard_map/all_gather | solution.py:33
  468.5 65.0 %reduce-scatter.25.cloned.1.call-start = ((), (), s32[]{:S(2)}) async-start(), calls=%async_computation.27 | async-start | bytes 3932160 | tf_op jit(solution)/shard_map/reduce_scatter | solution.py:50
  495.5 62.6 %all-gather.33.cloned.1.call-start = ((), (), s32[]{:S(2)}) async-start(), calls=%async_computation.28 | async-start | bytes 1966080 | tf_op jit(solution)/shard_map/all_gather | solution.py:33
  538.2 68.5 %reduce-scatter.27.cloned.1.call-start = ((), (), s32[]{:S(2)}) async-start(), calls=%async_computation.29 | async-start | bytes 3932160 | tf_op jit(solution)/shard_map/reduce_scatter | solution.py:37
  568.6 62.3 %all-gather.35.cloned.1.call-start = ((), (), s32[]{:S(2)}) async-start(), calls=%async_computation.30 | async-start | bytes 1966080 | tf_op jit(solution)/shard_map/all_gather | solution.py:33
  611.1 107.5 %reduce-scatter.29.cloned.1.call-start = ((), (), s32[]{:S(2)}) async-start(), calls=%async_computation.31 | async-start | bytes 3932160 | tf_op jit(solution)/shard_map/reduce_scatter | solution.py:37
  680.5 78.8 %reduce-scatter.35.cloned.1.call-start = ((), (), s32[]{:S(2)}) async-start(), calls=%async_computation.36 | async-start | bytes 3932160 | tf_op jit(solution)/shard_map/reduce_scatter | solution.py:37
  685.3 98.0 %all-gather.37.cloned.1.call-start = ((), (), s32[]{:S(2)}) async-start(), calls=%async_computation.32 | async-start | bytes 1966080 | tf_op jit(solution)/shard_map/all_gather | solution.py:33
  763.5 67.0 %reduce-scatter.31.cloned.1.call-start = ((), (), s32[]{:S(2)}) async-start(), calls=%async_computation.33 | async-start | bytes 3932160 | tf_op jit(solution)/shard_map/reduce_scatter | solution.py:37
  792.5 59.4 %all-gather.41.cloned.1.call-start = ((), (), s32[]{:S(2)}) async-start(), calls=%async_computation.37 | async-start | bytes 1966080 | tf_op jit(solution)/shard_map/all_gather | solution.py:33
  795.6 131.8 %all-gather.39.cloned.1.call-start = ((), (), s32[]{:S(2)}) async-start(), calls=%async_computation.34 | async-start | bytes 1966080 | tf_op jit(solution)/shard_map/all_gather | solution.py:33
  834.4 172.2 %reduce-scatter.41.cloned.1.call-start = ((), (), s32[]{:S(2)}) async-start(), calls=%async_computation.40 | async-start | bytes 2359296 | tf_op jit(solution)/shard_map/reduce_scatter | solution.py:411
  864.7 144.9 %reduce-scatter.43.cloned.1.call-start = ((), (), s32[]{:S(2)}) async-start(), calls=%async_computation.41 | async-start | bytes 294912
  927.2 214.9 %all-reduce.5.cloned.1.call-start = ((), (), s32[]{:S(2)}) async-start(), calls=%async_computation.42 | async-start | bytes 6291456
  979.8 252.6 %reduce-scatter.39.cloned.1.call-start = ((), (), s32[]{:S(2)}) async-start(), calls=%async_computation.39 | async-start | bytes 4718592 | tf_op jit(solution)/shard_map/reduce_scatter | solution.py:409
  995.6 277.2 %reduce-scatter.37.cloned.1.call-start = ((), (), s32[]{:S(2)}) async-start(), calls=%async_computation.38 | async-start | bytes 3932160 | tf_op jit(solution)/shard_map/reduce_scatter | solution.py:37
  1000.4 322.5 %reduce-scatter.33.cloned.1.call-start = ((), (), s32[]{:S(2)}) async-start(), calls=%async_computation.35 | async-start | bytes 3932160 | tf_op jit(solution)/shard_map/reduce_scatter | solution.py:37
  1004.7 311.1 %copy-start.68 = (f32[3,128,64]{1,2,0:T(8,128)S(1)}, f32[3,128,64]{1,2,0:T(8,128)}, u32[]{:S(2)}) copy-start(f32[3,128,64]{1,2,0:T(8,128)} %param.42) | copy-start | bytes 294916
  1004.7 312.8 %copy-start.60 = (f32[2,512,64]{1,2,0:T(8,128)S(1)}, f32[2,512,64]{1,2,0:T(8,128)}, u32[]{:S(2)}) copy-start(f32[2,512,64]{1,2,0:T(8,128)} %param.44) | copy-start | bytes 786436
  (113 other events, 4755.9 us)
Sparse Core Ops, SparseCore 0:
  10.8 44.4 all-gather.14
  56.8 18.5 all-gather.16
  106.9 37.9 reduce-scatter.16
  147.0 19.6 all-gather.24
  169.5 40.2 all-gather.20
  211.8 18.4 all-gather.18
  233.3 40.1 all-gather.22
  276.2 36.7 reduce-scatter.20
  315.5 37.9 reduce-scatter.18
  355.5 19.6 all-gather.26
  377.4 19.6 all-gather.28
  427.9 37.9 reduce-scatter.22
  468.7 19.6 all-gather.30
  495.6 37.9 reduce-scatter.24
  538.3 19.6 all-gather.32
  568.8 37.9 reduce-scatter.26
  611.2 19.6 all-gather.34
  680.6 37.9 reduce-scatter.28
  721.3 37.9 reduce-scatter.34
  763.7 19.6 all-gather.36
  792.6 37.9 reduce-scatter.30
  832.2 19.6 all-gather.40
  853.5 19.6 all-gather.38
  877.0 67.8 reduce-scatter.40
  949.2 60.2 reduce-scatter.42
  1013.5 128.5 all-reduce.4
  1145.5 86.8 reduce-scatter.38
  1235.1 37.7 reduce-scatter.36
  1275.4 38.2 reduce-scatter.32
where the time goes:
time: 1340 us; the launch traced here: 1330 us
  waiting for transfers between devices  776 us (58%)
  matrix products  248 us (19%)
  blocking collectives  109 us (8%)
  other arithmetic  94.7 us (7%)
  local copies, waits for them, and re-layouts  78.5 us (6%)
  between operations  21.7 us (2%)
    reduce_scatter x6, waiting for transfers between devices, sum_rows(): lax.psum_scatter(row_term(jnp.int32(0), row_count * lax.axis_size('mp')),...  183 us
    all_gather x11, waiting for transfers between devices, gather_rows(): return lax.all_gather(values, 'mp', axis=0, tiled=True)  170 us
    reduce_scatter x5, waiting for transfers between devices, forward_branch(): lax.psum_scatter(forward_term(operand, weights_local), 'mp', scatter_dime...  149 us
    unnamed x31, waiting for transfers between devices  127 us
    reduce_scatter x1, waiting for transfers between devices, on_device(): lax.psum_scatter(grad_in, 'dp', scatter_dimension=1, tiled=True)  86.9 us
    dot_general x18, matrix products, one_block(): jnp.einsum('bhd,khd->hbk', query_part, keys_all, preferred_element_type=j...  54.9 us
    psum x1, blocking collectives, on_device(): grad_norm = jnp.sqrt(lax.psum(squares, ('dp', 'mp')))  39.4 us
    all_gather x1, waiting for transfers between devices, on_device(): lax.all_gather(lowered[3], 'dp', axis=2, tiled=True)  39.1 us
  transfers between devices with their start and end apart: 29, of which 25 were waited for; matrix products, arithmetic and copies ran while one was open for 19% of the time, Pallas kernels for 0%

commit v1 on v0

v1 whole, which is shorter than its diff:
```python
import functools

import jax
import jax.numpy as jnp
from jax import lax
from jax.experimental import pallas as pl
from jax.experimental.pallas import tpu as pltpu
from jax.sharding import Mesh
from jax.sharding import PartitionSpec as P

HEAD_DIM = 64
STEP = 10
BLOCK = 128
PAIR = 2 * HEAD_DIM

norm_eps = 1e-05
beta_one = 0.9
beta_two = 0.98
adam_eps = 1e-08
weight_decay = 0.01
rate_matrix = 0.1
rate_norm = 0.5
clip_bound = 1.0
masked_score = -1e30
score_scale = HEAD_DIM ** (-0.5)
gelu_a = 0.7978845608028654
gelu_b = 0.044715

F32 = jnp.float32
BF16 = jnp.bfloat16
ANY = pl.ANY
SMEM = pltpu.SMEM
VMEM = pltpu.VMEM

NN = (((1,), (0,)), ((), ()))
NT = (((1,), (1,)), ((), ()))


def mm(a, b, dims=NN):
    return lax.dot_general(a, b, dims, preferred_element_type=F32)


def vmem(count=1):
    return [pl.BlockSpec(memory_space=VMEM)] * count


def params(mib):
    return pltpu.CompilerParams(vmem_limit_bytes=mib * 1024 * 1024)


def shaped(shape, dtype):
    return jax.ShapeDtypeStruct(shape, dtype)


def normalize(total):
    centred = total - jnp.mean(total, axis=-1, keepdims=True)
    spread = jnp.mean(centred * centred, axis=-1, keepdims=True)
    rstd = lax.rsqrt(spread + norm_eps)
    return centred * rstd, rstd


def norm_backward(grad_out, xhat, rstd, gain):
    scaled = grad_out * gain
    first = jnp.mean(scaled, axis=-1, keepdims=True)
    second = jnp.mean(scaled * xhat, axis=-1, keepdims=True)
    return rstd * (scaled - first - xhat * second)


def norm_param_grads(grad_out, xhat):
    return (
        jnp.sum(grad_out * xhat, axis=0, keepdims=True),
        jnp.sum(grad_out, axis=0, keepdims=True),
    )


def half_masks():
    lane = lax.broadcasted_iota(jnp.int32, (1, PAIR), 1)
    low = jnp.where(lane < HEAD_DIM, 1.0, 0.0).astype(BF16)
    high = jnp.where(lane < HEAD_DIM, 0.0, 1.0).astype(BF16)
    return low, high


def stack_pair(values, masks):
    return jnp.concatenate([values * masks[0], values * masks[1]], axis=0)


def weight_copies(w_hbm, w_vmem, sems):
    blocks, depth, width = w_hbm.shape
    part = width // 4
    copies = []
    for kind in range(4):
        copies.append([])
        for block in range(blocks):
            copies[kind].append(
                pltpu.make_async_copy(
                    w_hbm.at[block, :, pl.ds(kind * part, part)],
                    w_vmem.at[:, pl.ds((kind * blocks + block) * part, part)],
                    sems.at[kind, block],
                )
            )
    return copies


def grad_copies(dw_vmem, dw_hbm, sems):
    blocks, depth, width = dw_hbm.shape
    part = width // 4
    copies = []
    for kind in range(4):
        copies.append([])
        for block in range(blocks):
            copies[kind].append(
                pltpu.make_async_copy(
                    dw_vmem.at[:, pl.ds((kind * blocks + block) * part, part)],
                    dw_hbm.at[block, :, pl.ds(kind * part, part)],
                    sems.at[kind, block],
                )
            )
    return copies


def start_all(groups):
    for group in groups:
        for copy in group:
            copy.start()


def wait_all(group):
    for copy in group:
        copy.wait()


def self_forward_kernel(
    x_ref, segq_ref, segk_ref, w_hbm, norm_ref,
    xhat_ref, rstd_ref, q_ref, k_ref, v_ref, ctx_ref, pt_ref,
    w_vmem, vt_s, ctxt_s, sems,
):
    copies = weight_copies(w_hbm, w_vmem, sems)
    start_all([copies[1], copies[2], copies[0], copies[3]])
    rows, width = q_ref.shape
    blocks, pairs = rows // BLOCK, width // PAIR
    window = 3 * BLOCK
    wait_all(copies[1])
    wait_all(copies[2])
    kv = mm(x_ref[...], w_vmem[:, width : 3 * width]).astype(BF16)
    k_ref[...] = kv[:, :width]
    v_ref[...] = kv[:, width:]
    vt_s[...] = kv[:, width:].T
    wait_all(copies[0])
    q = mm(x_ref[BLOCK : BLOCK + rows, :], w_vmem[:, :width]).astype(BF16)
    q_ref[...] = q * jnp.asarray(score_scale, BF16)
    masks = half_masks()
    for block in range(blocks):
        at = pl.ds(block * BLOCK, BLOCK)
        keys_at = pl.ds(block * BLOCK, window)
        allowed = segk_ref[keys_at, :] == segq_ref[block : block + 1, :]
        for pair in range(pairs):
            cols = pl.ds(pair * PAIR, PAIR)
            stacked = stack_pair(q_ref[at, cols], masks)
            scores = mm(k_ref[keys_at, cols], stacked, NT)
            scores = jnp.where(allowed, scores, masked_score)
            highest = jnp.max(scores, axis=0, keepdims=True)
            raised = jnp.exp(scores - highest)
            total = jnp.sum(raised, axis=0, keepdims=True)
            probs = (raised * (1.0 / total)).astype(BF16)
            pt_ref[block * pairs + pair] = probs
            context = mm(vt_s[cols, keys_at], probs).astype(BF16)
            ctxt_s[pl.ds(pair * PAIR, HEAD_DIM), at] = context[:HEAD_DIM, :BLOCK]
            ctxt_s[pl.ds(pair * PAIR + HEAD_DIM, HEAD_DIM), at] = context[HEAD_DIM:, BLOCK:]
    context = ctxt_s[...].T
    ctx_ref[...] = context
    wait_all(copies[3])
    branch = mm(context, w_vmem[:, 3 * width :], NT)
    xhat, rstd = normalize(x_ref[BLOCK : BLOCK + rows, :].astype(F32) + branch)
    xhat_ref[...] = xhat
    rstd_ref[...] = rstd


def self_forward(x, segq, segk, weights, norm):
    keys, width = x.shape
    rows = keys - 2 * BLOCK
    blocks, pairs = rows // BLOCK, width // PAIR
    return pl.pallas_call(
        self_forward_kernel,
        out_shape=(
            shaped((rows, width), F32),
            shaped((rows, 1), F32),
            shaped((rows, width), BF16),
            shaped((keys, width), BF16),
            shaped((keys, width), BF16),
            shaped((rows, width), BF16),
            shaped((blocks * pairs, 3 * BLOCK, 2 * BLOCK), BF16),
        ),
        in_specs=vmem(3) + [pl.BlockSpec(memory_space=ANY)] + vmem(1),
        out_specs=tuple(vmem(7)),
        scratch_shapes=[
            pltpu.VMEM((width, 4 * width), BF16),
            pltpu.VMEM((width, keys), BF16),
            pltpu.VMEM((width, rows), BF16),
            pltpu.SemaphoreType.DMA((4, weights.shape[0])),
        ],
        compiler_params=params(32),
        name="self_forward",
    )(x, segq, segk, weights, norm)


def self_backward_kernel(
    dy_ref, xhat_ref, rstd_ref, norm_ref, w_hbm, x_ref, q_ref, k_ref, v_ref, ctx_ref, pt_ref,
    dx_ref, dnorm_ref, dw_hbm,
    w_vmem, dw_s, dctx_s, kt_s, dqt_s, dkv_s, sems, out_sems,
):
    copies = weight_copies(w_hbm, w_vmem, sems)
    start_all([copies[3], copies[0], copies[1], copies[2]])
    out_copies = grad_copies(dw_s, dw_hbm, out_sems)
    rows, width = q_ref.shape
    blocks, pairs = rows // BLOCK, width // PAIR
    window = 3 * BLOCK
    masks = half_masks()
    dy = dy_ref[...]
    xhat = xhat_ref[...]
    dgain, dshift = norm_param_grads(dy, xhat)
    dnorm_ref[0:1, :] = dgain
    dnorm_ref[1:2, :] = dshift
    dtotal = norm_backward(dy, xhat, rstd_ref[...], norm_ref[0:1, :])
    low = dtotal.astype(BF16)
    wait_all(copies[3])
    dctx_s[...] = mm(low, w_vmem[:, 3 * width :]).astype(BF16)
    dw_s[:, 3 * width :] = mm(low.T, ctx_ref[...]).astype(BF16)
    start_all([out_copies[3]])
    kt_s[...] = k_ref[...].T
    dkv_s[...] = jnp.zeros_like(dkv_s)
    for block in range(blocks):
        at = pl.ds(block * BLOCK, BLOCK)
        keys_at = pl.ds(block * BLOCK, window)
        for pair in range(pairs):
            cols = pl.ds(pair * PAIR, PAIR)
            dstacked = stack_pair(dctx_s[at, cols], masks)
            qstacked = stack_pair(q_ref[at, cols], masks)
            probs_low = pt_ref[block * pairs + pair]
            probs = probs_low.astype(F32)
            dprobs = mm(v_ref[keys_at, cols], dstacked, NT)
            delta = jnp.sum(probs * dprobs, axis=0, keepdims=True)
            dscores = (probs * (dprobs - delta)).astype(BF16)
            dkv_s[keys_at, cols] += mm(dscores, qstacked)
            dkv_s[keys_at, pl.ds(width + pair * PAIR, PAIR)] += mm(probs_low, dstacked)
            dqt = mm(kt_s[cols, keys_at], dscores) * score_scale
            dqt = dqt.astype(BF16)
            dqt_s[pl.ds(pair * PAIR, HEAD_DIM), at] = dqt[:HEAD_DIM, :BLOCK]
            dqt_s[pl.ds(pair * PAIR + HEAD_DIM, HEAD_DIM), at] = dqt[HEAD_DIM:, BLOCK:]
    dq = dqt_s[...].T
    dkv = dkv_s[...].astype(BF16)
    xt = x_ref[...].T
    dw_s[:, width : 3 * width] = mm(xt, dkv).astype(BF16)
    start_all([out_copies[1], out_copies[2]])
    dw_s[:, :width] = mm(xt[:, BLOCK : BLOCK + rows], dq).astype(BF16)
    start_all([out_copies[0]])
    wait_all(copies[1])
    wait_all(copies[2])
    dx_ref[...] = mm(dkv, w_vmem[:, width : 3 * width], NT)
    wait_all(copies[0])
    dx_ref[BLOCK : BLOCK + rows, :] += dtotal + mm(dq, w_vmem[:, :width], NT)
    for group in out_copies:
        wait_all(group)


def self_backward(dy, xhat, rstd, norm, weights, x, saved):
    keys, width = x.shape
    rows = keys - 2 * BLOCK
    mp = weights.shape[0]
    return pl.pallas_call(
        self_backward_kernel,
        out_shape=(
            shaped((keys, width), F32),
            shaped((2, width), F32),
            shaped(weights.shape, BF16),
        ),
        in_specs=vmem(4) + [pl.BlockSpec(memory_space=ANY)] + vmem(6),
        out_specs=(*vmem(2), pl.BlockSpec(memory_space=ANY)),
        scratch_shapes=[
            pltpu.VMEM((width, 4 * width), BF16),
            pltpu.VMEM((width, 4 * width), BF16),
            pltpu.VMEM((rows, width), BF16),
            pltpu.VMEM((width, keys), BF16),
            pltpu.VMEM((width, rows), BF16),
            pltpu.VMEM((keys, 2 * width), F32),
            pltpu.SemaphoreType.DMA((4, mp)),
            pltpu.SemaphoreType.DMA((4, mp)),
        ],
        compiler_params=params(40),
        name="self_backward",
    )(dy, xhat, rstd, norm, weights, x, *saved)


def cross_forward_kernel(
    range_ref, xin_ref, norm_in_ref, m_ref, segq_ref, segk_ref, w_hbm,
    xhat_ref, rstd_ref, q_ref, k_ref, v_ref, ctx_ref, lse_ref,
    w_vmem, vt_s, s_s, acc_s, ctxt_s, sems,
):
    copies = weight_copies(w_hbm, w_vmem, sems)
    start_all([copies[0], copies[1], copies[2], copies[3]])
    rows, width = q_ref.shape
    blocks, pairs = rows // BLOCK, width // PAIR
    masks = half_masks()
    inputs = xin_ref[...] * norm_in_ref[0:1, :] + norm_in_ref[1:2, :]
    wait_all(copies[0])
    q = mm(inputs.astype(BF16), w_vmem[:, :width]).astype(BF16)
    q_ref[...] = q * jnp.asarray(score_scale, BF16)
    wait_all(copies[1])
    wait_all(copies[2])

    @pl.loop(range_ref[0], range_ref[2 * blocks - 1])
    def _(key_block):
        keys_at = pl.ds(pl.multiple_of(key_block * BLOCK, BLOCK), BLOCK)
        kv = mm(m_ref[keys_at, :], w_vmem[:, width : 3 * width]).astype(BF16)
        k_ref[keys_at, :] = kv[:, :width]
        v_ref[keys_at, :] = kv[:, width:]
        vt_s[:, keys_at] = kv[:, width:].T

    for block in range(blocks):
        at = pl.ds(block * BLOCK, BLOCK)
        first, last = range_ref[2 * block], range_ref[2 * block + 1]
        stacked = [stack_pair(q_ref[at, pl.ds(p * PAIR, PAIR)], masks) for p in range(pairs)]
        segq = segq_ref[block : block + 1, :]

        def scan_scores(key_block, highest):
            keys_at = pl.ds(pl.multiple_of(key_block * BLOCK, BLOCK), BLOCK)
            allowed = segk_ref[keys_at, :] == segq
            result = []
            for pair in range(pairs):
                scores = mm(k_ref[keys_at, pl.ds(pair * PAIR, PAIR)], stacked[pair], NT)
                scores = jnp.where(allowed, scores, masked_score)
                s_s[pair, keys_at, :] = scores
                result.append(
                    jnp.maximum(highest[pair], jnp.max(scores, axis=0, keepdims=True))
                )
            return tuple(result)

        start = tuple(jnp.full((1, 2 * BLOCK), masked_score, F32) for _ in range(pairs))
        highest = lax.fori_loop(first, last, scan_scores, start)
        acc_s[...] = jnp.zeros_like(acc_s)

        def scan_context(key_block, sums):
            keys_at = pl.ds(pl.multiple_of(key_block * BLOCK, BLOCK), BLOCK)
            result = []
            for pair in range(pairs):
                raised = jnp.exp(s_s[pair, keys_at, :] - highest[pair])
                result.append(sums[pair] + jnp.sum(raised, axis=0, keepdims=True))
                acc_s[pair] += mm(vt_s[pl.ds(pair * PAIR, PAIR), keys_at], raised.astype(BF16))
            return tuple(result)

        start = tuple(jnp.zeros((1, 2 * BLOCK), F32) for _ in range(pairs))
        sums = lax.fori_loop(first, last, scan_context, start)
        for pair in range(pairs):
            context = (acc_s[pair] * (1.0 / sums[pair])).astype(BF16)
            ctxt_s[pl.ds(pair * PAIR, HEAD_DIM), at] = context[:HEAD_DIM, :BLOCK]
            ctxt_s[pl.ds(pair * PAIR + HEAD_DIM, HEAD_DIM), at] = context[HEAD_DIM:, BLOCK:]
            row = block * pairs + pair
            lse_ref[row : row + 1, :] = highest[pair] + jnp.log(sums[pair])
    context = ctxt_s[...].T
    ctx_ref[...] = context
    wait_all(copies[3])
    branch = mm(context, w_vmem[:, 3 * width :], NT)
    xhat, rstd = normalize(inputs + branch)
    xhat_ref[...] = xhat
    rstd_ref[...] = rstd


def cross_forward(ranges, xin, norm_in, memory, segq, segk, weights):
    rows, width = xin.shape
    keys = memory.shape[0]
    blocks, pairs = rows // BLOCK, width // PAIR
    return pl.pallas_call(
        cross_forward_kernel,
        out_shape=(
            shaped((rows, width), F32),
            shaped((rows, 1), F32),
            shaped((rows, width), BF16),
            shaped((keys, width), BF16),
            shaped((keys, width), BF16),
            shaped((rows, width), BF16),
            shaped((blocks * pairs, 2 * BLOCK), F32),
        ),
        in_specs=[pl.BlockSpec(memory_space=SMEM)]
        + vmem(5)
        + [pl.BlockSpec(memory_space=ANY)],
        out_specs=tuple(vmem(7)),
        scratch_shapes=[
            pltpu.VMEM((width, 4 * width), BF16),
            pltpu.VMEM((width, keys), BF16),
            pltpu.VMEM((pairs, keys, 2 * BLOCK), F32),
            pltpu.VMEM((pairs, PAIR, 2 * BLOCK), F32),
            pltpu.VMEM((width, rows), BF16),
            pltpu.SemaphoreType.DMA((4, weights.shape[0])),
        ],
        compiler_params=params(40),
        name="cross_forward",
    )(ranges, xin, norm_in, memory, segq, segk, weights)


def cross_backward_kernel(
    range_ref, dy_ref, xhat_ref, rstd_ref, norm_ref, xin_ref, norm_in_ref, m_ref,
    segq_ref, segk_ref, q_ref, k_ref, v_ref, ctx_ref, lse_ref, w_hbm,
    dx_ref, dm_ref, dnorm_ref, dw_hbm,
    w_vmem, dw_s, dctx_s, kt_s, dqt_acc, dqt_s, dkv_s, dwkv_s, sems, out_sems,
):
    copies = weight_copies(w_hbm, w_vmem, sems)
    start_all([copies[3], copies[0], copies[1], copies[2]])
    out_copies = grad_copies(dw_s, dw_hbm, out_sems)
    rows, width = q_ref.shape
    blocks, pairs = rows // BLOCK, width // PAIR
    heads_here = width // HEAD_DIM
    masks = half_masks()
    dy = dy_ref[...]
    xhat = xhat_ref[...]
    dgain, dshift = norm_param_grads(dy, xhat)
    dnorm_ref[0:1, :] = dgain
    dnorm_ref[1:2, :] = dshift
    dtotal = norm_backward(dy, xhat, rstd_ref[...], norm_ref[0:1, :])
    low = dtotal.astype(BF16)
    wait_all(copies[3])
    dctx = mm(low, w_vmem[:, 3 * width :]).astype(BF16)
    dctx_s[...] = dctx
    dw_s[:, 3 * width :] = mm(low.T, ctx_ref[...]).astype(BF16)
    start_all([out_copies[3]])
    products = (dctx.astype(F32) * ctx_ref[...].astype(F32)).T
    deltas = [
        jnp.sum(products[h * HEAD_DIM : (h + 1) * HEAD_DIM, :], axis=0, keepdims=True)
        for h in range(heads_here)
    ]
    everything_first, everything_last = range_ref[0], range_ref[2 * blocks - 1]

    @pl.loop(everything_first, everything_last)
    def _(key_block):
        keys_at = pl.ds(pl.multiple_of(key_block * BLOCK, BLOCK), BLOCK)
        kt_s[:, keys_at] = k_ref[keys_at, :].T
        dkv_s[keys_at, :] = jnp.zeros((BLOCK, 2 * width), F32)

    for block in range(blocks):
        at = pl.ds(block * BLOCK, BLOCK)
        lanes = slice(block * BLOCK, (block + 1) * BLOCK)
        first, last = range_ref[2 * block], range_ref[2 * block + 1]
        qstacked = [stack_pair(q_ref[at, pl.ds(p * PAIR, PAIR)], masks) for p in range(pairs)]
        dstacked = [stack_pair(dctx_s[at, pl.ds(p * PAIR, PAIR)], masks) for p in range(pairs)]
        delta = [
            jnp.concatenate([deltas[2 * p][:, lanes], deltas[2 * p + 1][:, lanes]], axis=1)
            for p in range(pairs)
        ]
        segq = segq_ref[block : block + 1, :]
        dqt_acc[...] = jnp.zeros_like(dqt_acc)

        @pl.loop(first, last)
        def _(key_block):
            keys_at = pl.ds(pl.multiple_of(key_block * BLOCK, BLOCK), BLOCK)
            allowed = segk_ref[keys_at, :] == segq
            for pair in range(pairs):
                cols = pl.ds(pair * PAIR, PAIR)
                row = block * pairs + pair
                scores = mm(k_ref[keys_at, cols], qstacked[pair], NT)
                scores = jnp.where(allowed, scores, masked_score)
                probs = jnp.exp(scores - lse_ref[row : row + 1, :])
                dprobs = mm(v_ref[keys_at, cols], dstacked[pair], NT)
                dscores = (probs * (dprobs - delta[pair])).astype(BF16)
                dkv_s[keys_at, cols] += mm(dscores, qstacked[pair])
                dkv_s[keys_at, pl.ds(width + pair * PAIR, PAIR)] += mm(
                    probs.astype(BF16), dstacked[pair]
                )
                dqt_acc[pair] += mm(kt_s[cols, keys_at], dscores)

        for pair in range(pairs):
            dqt = (dqt_acc[pair] * score_scale).astype(BF16)
            dqt_s[pl.ds(pair * PAIR, HEAD_DIM), at] = dqt[:HEAD_DIM, :BLOCK]
            dqt_s[pl.ds(pair * PAIR + HEAD_DIM, HEAD_DIM), at] = dqt[HEAD_DIM:, BLOCK:]
    dq = dqt_s[...].T
    inputs = (xin_ref[...] * norm_in_ref[0:1, :] + norm_in_ref[1:2, :]).astype(BF16)
    dw_s[:, :width] = mm(inputs.T, dq).astype(BF16)
    start_all([out_copies[0]])
    wait_all(copies[0])
    dx_ref[...] = dtotal + mm(dq, w_vmem[:, :width], NT)
    wait_all(copies[1])
    wait_all(copies[2])
    dm_ref[...] = jnp.zeros_like(dm_ref)
    dwkv_s[...] = jnp.zeros_like(dwkv_s)

    @pl.loop(everything_first, everything_last)
    def _(key_block):
        keys_at = pl.ds(pl.multiple_of(key_block * BLOCK, BLOCK), BLOCK)
        dkv = dkv_s[keys_at, :].astype(BF16)
        dm_ref[keys_at, :] = mm(dkv, w_vmem[:, width : 3 * width], NT).astype(BF16)
        dwkv_s[...] += mm(m_ref[keys_at, :].T, dkv)

    dw_s[:, width : 3 * width] = dwkv_s[...].astype(BF16)
    start_all([out_copies[1], out_copies[2]])
    for group in out_copies:
        wait_all(group)


def cross_backward(ranges, dy, xhat, rstd, norm, xin, norm_in, memory, segq, segk, saved, weights):
    rows, width = xin.shape
    keys = memory.shape[0]
    pairs = width // PAIR
    mp = weights.shape[0]
    return pl.pallas_call(
        cross_backward_kernel,
        out_shape=(
            shaped((rows, width), F32),
            shaped((keys, width), BF16),
            shaped((2, width), F32),
            shaped(weights.shape, BF16),
        ),
        in_specs=[pl.BlockSpec(memory_space=SMEM)]
        + vmem(14)
        + [pl.BlockSpec(memory_space=ANY)],
        out_specs=(*vmem(3), pl.BlockSpec(memory_space=ANY)),
        scratch_shapes=[
            pltpu.VMEM((width, 4 * width), BF16),
            pltpu.VMEM((width, 4 * width), BF16),
            pltpu.VMEM((rows, width), BF16),
            pltpu.VMEM((width, keys), BF16),
            pltpu.VMEM((pairs, PAIR, 2 * BLOCK), F32),
            pltpu.VMEM((width, rows), BF16),
            pltpu.VMEM((keys, 2 * width), F32),
            pltpu.VMEM((width, 2 * width), F32),
            pltpu.SemaphoreType.DMA((4, mp)),
            pltpu.SemaphoreType.DMA((4, mp)),
        ],
        compiler_params=params(48),
        name="cross_backward",
    )(ranges, dy, xhat, rstd, norm, xin, norm_in, memory, segq, segk, *saved, weights)


def feed_forward_kernel(
    xin_ref, norm_in_ref, norm_ref, w_ref,
    xhat_ref, rstd_ref, out_ref, hidden_ref, slope_ref,
    low_s, acc_s,
):
    step = pl.program_id(0)
    half = w_ref.shape[2] // 2

    @pl.when(step == 0)
    def _():
        inputs = xin_ref[...] * norm_in_ref[0:1, :] + norm_in_ref[1:2, :]
        low_s[...] = inputs.astype(BF16)
        acc_s[...] = inputs

    pre = mm(low_s[...], w_ref[0, :, :half])
    square = pre * pre
    tanh = jnp.tanh(gelu_a * pre * (1.0 + gelu_b * square))
    cdf = 0.5 + 0.5 * tanh
    hidden = (pre * cdf).astype(BF16)
    hidden_ref[...] = hidden
    slope = cdf + (0.5 * gelu_a) * pre * (1.0 - tanh * tanh) * (1.0 + (3.0 * gelu_b) * square)
    slope_ref[...] = slope.astype(BF16)
    acc_s[...] += mm(hidden, w_ref[0, :, half:], NT)

    @pl.when(step == pl.num_programs(0) - 1)
    def _():
        xhat, rstd = normalize(acc_s[...])
        xhat_ref[...] = xhat
        rstd_ref[...] = rstd
        out_ref[...] = (xhat * norm_ref[0:1, :] + norm_ref[1:2, :]).astype(BF16)


def feed_forward(xin, norm_in, norm, weights):
    rows, width = xin.shape
    mp, _, both = weights.shape
    half = both // 2
    whole = pl.BlockSpec((rows, width), lambda i: (0, 0))
    two = pl.BlockSpec((2, width), lambda i: (0, 0))
    part = pl.BlockSpec((rows, half), lambda i: (0, i))
    return pl.pallas_call(
        feed_forward_kernel,
        grid=(mp,),
        out_shape=(
            shaped((rows, width), F32),
            shaped((rows, 1), F32),
            shaped((rows, width), BF16),
            shaped((rows, mp * half), BF16),
            shaped((rows, mp * half), BF16),
        ),
        in_specs=[whole, two, two, pl.BlockSpec((1, width, both), lambda i: (i, 0, 0))],
        out_specs=(whole, pl.BlockSpec((rows, 1), lambda i: (0, 0)), whole, part, part),
        scratch_shapes=[pltpu.VMEM((rows, width), BF16), pltpu.VMEM((rows, width), F32)],
        compiler_params=params(32),
        name="feed_forward",
    )(xin, norm_in, norm, weights)


def feed_backward_kernel(
    dy_ref, xhat_ref, rstd_ref, norm_ref, xin_ref, norm_in_ref, w_ref, hidden_ref, slope_ref,
    dx_ref, dnorm_ref, dw_ref,
    low_s, lowt_s, xt_s,
):
    step = pl.program_id(0)
    half = w_ref.shape[2] // 2

    @pl.when(step == 0)
    def _():
        dy = dy_ref[...].astype(F32)
        xhat = xhat_ref[...]
        dgain, dshift = norm_param_grads(dy, xhat)
        dnorm_ref[0:1, :] = dgain
        dnorm_ref[1:2, :] = dshift
        dtotal = norm_backward(dy, xhat, rstd_ref[...], norm_ref[0:1, :])
        dx_ref[...] = dtotal
        low = dtotal.astype(BF16)
        low_s[...] = low
        lowt_s[...] = low.T
        inputs = xin_ref[...] * norm_in_ref[0:1, :] + norm_in_ref[1:2, :]
        xt_s[...] = inputs.astype(BF16).T

    dhidden = mm(low_s[...], w_ref[0, :, half:])
    dpre = (dhidden * slope_ref[...].astype(F32)).astype(BF16)
    dw_ref[0, :, :half] = mm(xt_s[...], dpre).astype(BF16)
    dw_ref[0, :, half:] = mm(lowt_s[...], hidden_ref[...]).astype(BF16)
    dx_ref[...] += mm(dpre, w_ref[0, :, :half], NT)


def feed_backward(dy, xhat, rstd, norm, xin, norm_in, weights, hidden, slope):
    rows, width = xin.shape
    mp, _, both = weights.shape
    half = both // 2
    whole = pl.BlockSpec((rows, width), lambda i: (0, 0))
    two = pl.BlockSpec((2, width), lambda i: (0, 0))
    part = pl.BlockSpec((rows, half), lambda i: (0, i))
    blocks = pl.BlockSpec((1, width, both), lambda i: (i, 0, 0))
    return pl.pallas_call(
        feed_backward_kernel,
        grid=(mp,),
        out_shape=(
            shaped((rows, width), F32),
            shaped((2, width), F32),
            shaped(weights.shape, BF16),
        ),
        in_specs=[
            whole, whole, pl.BlockSpec((rows, 1), lambda i: (0, 0)), two, whole, two,
            blocks, part, part,
        ],
        out_specs=(whole, two, blocks),
        scratch_shapes=[
            pltpu.VMEM((rows, width), BF16),
            pltpu.VMEM((width, rows), BF16),
            pltpu.VMEM((width, rows), BF16),
        ],
        compiler_params=params(32),
        name="feed_backward",
    )(dy, xhat, rstd, norm, xin, norm_in, weights, hidden, slope)


DP = ("z", "x")
MP = ("y", "c")
ALL = ("z", "x", "y", "c")


def gather_weights(shard):
    gathered = lax.all_gather(shard, MP + DP, axis=0, tiled=True)
    blocks = lax.axis_size(MP)
    return gathered.reshape(blocks, gathered.shape[0] // blocks, shard.shape[1])


def scatter_grads(grads):
    part = lax.psum_scatter(grads, MP, scatter_dimension=0, tiled=True)
    return lax.psum_scatter(part[0], DP, scatter_dimension=0, tiled=True)


def shift_rows(values, step):
    count = lax.axis_size(MP)
    pairs = [(i, i + step) for i in range(count) if 0 <= i + step < count]
    return lax.ppermute(values, MP, pairs)


def with_halos(values):
    before = shift_rows(values[-BLOCK:], 1)
    after = shift_rows(values[:BLOCK], -1)
    return jnp.concatenate([before, values, after], axis=0)


def add_halos(values):
    rows = values.shape[0] - 2 * BLOCK
    own = values[BLOCK : BLOCK + rows]
    after = shift_rows(values[:BLOCK], -1)
    before = shift_rows(values[BLOCK + rows :], 1)
    spread = jnp.pad(before, ((0, rows - BLOCK), (0, 0))) + jnp.pad(
        after, ((rows - BLOCK, 0), (0, 0))
    )
    return own + spread


def adam_step(weights, first, second, grads, rate, decay):
    first_new = beta_one * first + (1.0 - beta_one) * grads
    second_new = beta_two * second + (1.0 - beta_two) * grads * grads
    first_hat = first_new / (1.0 - beta_one**STEP)
    second_hat = second_new / (1.0 - beta_two**STEP)
    weights_new = weights - rate * (first_hat / (jnp.sqrt(second_hat) + adam_eps) + decay * weights)
    return (weights_new, first_new, second_new)


def on_device(
    encoder_input, decoder_copy, decoder_target, decoder_cotangent,
    source_segments, target_segments, glance_mask,
    attention_in, attention_out, feed_in, feed_out, norm_params,
    attention_in_first, attention_out_first, feed_in_first, feed_out_first, norm_params_first,
    attention_in_second, attention_out_second, feed_in_second, feed_out_second, norm_params_second,
):
    rows, width = encoder_input.shape
    length = source_segments.shape[1]
    masters = (attention_in, attention_out, feed_in, feed_out, norm_params)

    picked = glance_mask[0] == 1
    decoder_input = jnp.where(picked[:, None], decoder_target, decoder_copy)
    encoder_x = with_halos(encoder_input)
    decoder_x = with_halos(decoder_input)

    def attention_shard(number):
        parts = [attention_in[3 * number + kind] for kind in range(3)]
        return jnp.concatenate(parts + [attention_out[number].T], axis=1).astype(BF16)

    def feed_shard(number):
        return jnp.concatenate([feed_in[number], feed_out[number].T], axis=1).astype(BF16)

    norms = lax.all_gather(norm_params.astype(BF16), DP, axis=2, tiled=True).astype(F32)
    w_enc = gather_weights(attention_shard(0))
    w_enc_feed = gather_weights(feed_shard(0))
    w_self = gather_weights(attention_shard(1))
    w_cross = gather_weights(attention_shard(2))
    w_dec_feed = gather_weights(feed_shard(1))

    position = lax.axis_index(MP) * rows
    blocks = rows // BLOCK

    def query_segments(row):
        own = lax.dynamic_slice(row, (position,), (rows,)).reshape(blocks, BLOCK)
        return jnp.concatenate([own, own], axis=1)

    def key_segments(row):
        padded = jnp.pad(row, (BLOCK, BLOCK), constant_values=-1)
        return lax.dynamic_slice(padded, (position,), (rows + 2 * BLOCK,))[:, None]

    source_row, target_row = source_segments[0], target_segments[0]
    source_q, target_q = query_segments(source_row), query_segments(target_row)
    source_k, target_k = key_segments(source_row), key_segments(target_row)
    lowest, highest = target_q[:, 0], target_q[:, BLOCK - 1]
    first_key = jnp.sum((source_row[None, :] < lowest[:, None]).astype(jnp.int32), axis=1)
    last_key = jnp.sum((source_row[None, :] <= highest[:, None]).astype(jnp.int32), axis=1)
    ranges = jnp.stack([first_key // BLOCK, (last_key + BLOCK - 1) // BLOCK], axis=1)
    ranges = ranges.astype(jnp.int32).reshape(2 * blocks)

    xhat0, rstd0, *enc_saved = self_forward(encoder_x, source_q, source_k, w_enc, norms[0])
    xhat1, rstd1, encoder_output, enc_hidden, enc_slope = feed_forward(
        xhat0, norms[0], norms[1], w_enc_feed
    )
    memory = lax.all_gather(encoder_output, MP, axis=0, tiled=True)
    xhat2, rstd2, *self_saved = self_forward(decoder_x, target_q, target_k, w_self, norms[2])
    xhat3, rstd3, *cross_saved = cross_forward(
        ranges, xhat2, norms[2], memory, target_q, source_row[:, None], w_cross
    )
    xhat4, rstd4, decoder_output, dec_hidden, dec_slope = feed_forward(
        xhat3, norms[3], norms[4], w_dec_feed
    )

    d4, dnorm4, dw_dec_feed = feed_backward(
        decoder_cotangent, xhat4, rstd4, norms[4], xhat3, norms[3], w_dec_feed, dec_hidden, dec_slope
    )
    g_dec_feed = scatter_grads(dw_dec_feed)
    d3, dmemory, dnorm3, dw_cross = cross_backward(
        ranges, d4, xhat3, rstd3, norms[3], xhat2, norms[2], memory,
        target_q, source_row[:, None], cross_saved, w_cross,
    )
    dmemory = lax.psum_scatter(dmemory, MP, scatter_dimension=0, tiled=True)
    g_cross = scatter_grads(dw_cross)
    dx_dec, dnorm2, dw_self = self_backward(
        d3, xhat2, rstd2, norms[2], w_self, decoder_x, self_saved
    )
    g_self = scatter_grads(dw_self)
    d1, dnorm1, dw_enc_feed = feed_backward(
        dmemory, xhat1, rstd1, norms[1], xhat0, norms[0], w_enc_feed, enc_hidden, enc_slope
    )
    g_enc_feed = scatter_grads(dw_enc_feed)
    dx_enc, dnorm0, dw_enc = self_backward(
        d1, xhat0, rstd0, norms[0], w_enc, encoder_x, enc_saved
    )
    g_enc = scatter_grads(dw_enc)
    decoder_input_grad = add_halos(dx_dec)
    encoder_input_grad = add_halos(dx_enc)

    dnorms = lax.psum(jnp.stack([dnorm0, dnorm1, dnorm2, dnorm3, dnorm4]), MP)
    g_norms = lax.psum_scatter(dnorms, DP, scatter_dimension=2, tiled=True)

    attention_parts = [g.astype(F32) for g in (g_enc, g_self, g_cross)]
    feed_parts = [g.astype(F32) for g in (g_enc_feed, g_dec_feed)]
    squares = sum(jnp.sum(g * g) for g in attention_parts + feed_parts)
    squares = squares + jnp.sum(g_norms * g_norms) / lax.axis_size(MP)
    grad_norm = jnp.sqrt(lax.psum(squares, ALL))
    factor = clip_bound / jnp.maximum(grad_norm, clip_bound)

    part = attention_in.shape[2]
    half = feed_in.shape[2]
    g_in = jnp.stack(
        [g[:, kind * part : (kind + 1) * part] for g in attention_parts for kind in range(3)]
    )
    g_out = jnp.stack([g[:, 3 * part :].T for g in attention_parts])
    g_first = jnp.stack([g[:, :half] for g in feed_parts])
    g_second = jnp.stack([g[:, half:].T for g in feed_parts])
    reduced = (g_in, g_out, g_first, g_second, g_norms)
    firsts = (
        attention_in_first, attention_out_first, feed_in_first, feed_out_first, norm_params_first,
    )
    seconds = (
        attention_in_second, attention_out_second, feed_in_second, feed_out_second,
        norm_params_second,
    )
    results = []
    for number in range(5):
        rate = rate_norm if number == 4 else rate_matrix
        decay = 0.0 if number == 4 else weight_decay
        results.append(
            adam_step(
                masters[number], firsts[number], seconds[number], reduced[number] * factor, rate, decay
            )
        )
    return (
        encoder_output,
        decoder_output,
        encoder_input_grad,
        decoder_input_grad,
        grad_norm,
        *(result[0] for result in results),
        *(result[1] for result in results),
        *(result[2] for result in results),
    )


def solution(mesh):
    dp, mp = mesh.shape["dp"], mesh.shape["mp"]
    fine = Mesh(mesh.devices.reshape(dp // 2, 2, mp // 2, 2), ALL)
    tokens = P(ALL, None)
    columns = P(None, DP, MP)
    turned = P(None, MP, DP)
    states = (columns, turned, columns, turned, P(None, None, DP))
    return jax.shard_map(
        on_device,
        mesh=fine,
        in_specs=(
            *((tokens,) * 4),
            P(DP, None),
            P(DP, None),
            P(DP, MP),
            *states,
            *states,
            *states,
        ),
        out_specs=(*((tokens,) * 4), P(), *states, *states, *states),
        check_vma=False,
    )
```

time: 1340 us -> 1060 us (0.79)
  matrix products: 248 us -> 0 us
  Pallas kernels: 0 us -> 87.6 us
  other arithmetic: 94.7 us -> 27.8 us
  blocking collectives: 109 us -> 78.9 us
  waiting for transfers between devices: 776 us -> 756 us
  local copies, waits for them, and re-layouts: 78.5 us -> 60.6 us
  starting transfers between devices: 3.1 us -> 16.8 us
    dot_general x104 -> x0, matrix products: 244 us -> none  [the longest x18 54.9 us: one_block(): jnp.einsum('bhd,khd->hbk', query_part, keys_all, preferred_element_type=j...]
    pallas_call x0 -> x10, Pallas kernels: none -> 87.6 us  [the longest x1 20.3 us: cross_backward(): pl.pallas_call(cross_backward_kernel, out_shape=(shaped((rows, width), F3...]
    unnamed x31 -> x19, waiting for transfers between devices: 127 us -> 61 us
    reduce_scatter x13 -> x11, waiting for transfers between devices: 418 us -> 469 us  [the longest x5 309 us: scatter_grads(): return lax.psum_scatter(part[0], DP, scatter_dimension=0, tiled=True)]
    reduce_sum x33 -> x7, other arithmetic: 44.2 us -> 8.43 us  [the longest x5 7.59 us: on_device(): squares = sum((jnp.sum(g * g) for g in attention_parts + feed_parts))]
    unnamed x244 -> x192, local copies, waits for them, and re-layouts: 26.5 us -> 58.3 us
    all_gather x2 -> x1, blocking collectives: 64.1 us -> 32.9 us  [on_device(): lax.all_gather(norm_params.astype(BF16), DP, axis=2, tiled=True).astype(F32)]
    slice x8 -> x5, local copies, waits for them, and re-layouts: 20.7 us -> 0.98 us  [the longest x2 0.77 us: add_halos(): before = shift_rows(values[BLOCK + rows:], 1)]
  transfers between devices with their start and end apart: 29 -> 26, of which waited for: 25 -> 19; matrix products, arithmetic and copies ran while one was open for 19% -> 3% of each run, Pallas kernels for 0% -> 5%
where the time goes in v1:
time: 1060 us; the launch traced here: 1050 us
  waiting for transfers between devices  756 us (71%)
  Pallas kernels  87.6 us (8%)
  blocking collectives  78.9 us (7%)
  local copies, waits for them, and re-layouts  60.6 us (6%)
  other arithmetic  27.8 us (3%)
  between operations  21.3 us (2%)
  starting transfers between devices  16.8 us (2%)
    reduce_scatter x5, waiting for transfers between devices, scatter_grads(): return lax.psum_scatter(part[0], DP, scatter_dimension=0, tiled=True)  309 us
    all_gather x5, waiting for transfers between devices, gather_weights(): gathered = lax.all_gather(shard, MP + DP, axis=0, tiled=True)  203 us
    reduce_scatter x5, waiting for transfers between devices, scatter_grads(): part = lax.psum_scatter(grads, MP, scatter_dimension=0, tiled=True)  156 us
    unnamed x19, waiting for transfers between devices  61 us
    unnamed x192, local copies, waits for them, and re-layouts  58.3 us
    psum x1, blocking collectives, on_device(): grad_norm = jnp.sqrt(lax.psum(squares, ALL))  40 us
    all_gather x1, blocking collectives, on_device(): lax.all_gather(norm_params.astype(BF16), DP, axis=2, tiled=True).astype(F32)  32.9 us
  transfers between devices with their start and end apart: 26, of which 19 were waited for; matrix products, arithmetic and copies ran while one was open for 3% of the time, Pallas kernels for 5%

profile of v1, /device:TPU:0, one launch (start us, length us, event | category | flops | bytes accessed | tf_op | source)
XLA Modules:
  0.0 1048.6 jit_solution(14686680481437697358)
XLA Ops:
  14.6 3.0 collective-permute-start
  17.8 32.9 %all_gather.22 = bf16[5,2,512]{0,1,2:T(2,128)(2,1)S(1)} all-gather(bf16[5,2,64]{0,1,2:T(2,128)(2,1)S(1)} %copy.62), channel_id=1, replica_groups=mesh['z'=4,'x'=2,'y'=2,'c'=2] {'z','x'}, dimensions={2}, use_global_device_ids=true | all-gather | bytes 11520 | tf_op jit(solution)/shard_map/all_gather | solution.py:719
  51.3 20.0 %all-gather.7.cloned.1.call-done = bf16[2048,512]{1,0:T(8,128)(2,1)} async-done(((bf16[64,512]{1,0:T(8,128)(2,1)}), bf16[2048,512]{1,0:T(8,128)(2,1)}) %all-gather.7.cloned.1.call-update) | async-done | bytes 2097168 | tf_op jit(solution)/shard_map/all_gather | solution.py:654
  72.9 8.0 self_forward.2
  86.2 49.7 %all-gather.9.cloned.1.call-done = bf16[2048,1024]{1,0:T(8,128)(2,1)} async-done(((bf16[64,1024]{1,0:T(8,128)(2,1)}), bf16[2048,1024]{1,0:T(8,128)(2,1)}) %all-gather.9.cloned.1.call-update) | async-done | bytes 4194320 | tf_op jit(solution)/shard_map/all_gather | solution.py:654
  138.1 5.3 feed_forward.2
  154.6 40.0 %all-gather.11.cloned.1.call-done = bf16[2048,512]{1,0:T(8,128)(2,1)} async-done(((bf16[64,512]{1,0:T(8,128)(2,1)}), bf16[2048,512]{1,0:T(8,128)(2,1)}) %all-gather.11.cloned.1.call-update) | async-done | bytes 2097168 | tf_op jit(solution)/shard_map/all_gather | solution.py:654
  196.2 8.0 self_forward.3
  209.5 43.9 %all-gather.15.cloned.1.call-done = bf16[2048,512]{1,0:T(8,128)(2,1)} async-done(((bf16[64,512]{1,0:T(8,128)(2,1)}), bf16[2048,512]{1,0:T(8,128)(2,1)}) %all-gather.15.cloned.1.call-update) | async-done | bytes 2097168 | tf_op jit(solution)/shard_map/all_gather | solution.py:654
  253.4 20.5 %all-gather.13.cloned.1.call-done.m_ref = bf16[1536,512]{1,0:T(8,128)(2,1)} async-done(((bf16[384,512]{1,0:T(8,128)(2,1)}), bf16[1536,512]{1,0:T(8,128)(2,1)}) %all-gather.13.cloned.1.call-update) | async-done | bytes 1572880 | tf_op jit(solution)/shard_map/all_gather | solution.py:750
  276.9 9.0 cross_forward.1
  289.7 49.8 %all-gather.17.cloned.1.call-done = bf16[2048,1024]{1,0:T(8,128)(2,1)} async-done(((bf16[64,1024]{1,0:T(8,128)(2,1)}), bf16[2048,1024]{1,0:T(8,128)(2,1)}) %all-gather.17.cloned.1.call-update) | async-done | bytes 4194320 | tf_op jit(solution)/shard_map/all_gather | solution.py:654
  341.7 5.3 feed_forward.3
  347.0 5.8 feed_backward.2
  354.8 20.3 %cross_backward.1 = (f32[384,512]{1,0:T(8,128)S(1)}, bf16[1536,512]{1,0:T(8,128)(2,1)}, f32[2,512]{1,0:T(2,128)S(1)}, bf16[4,512,512]{2,1,0:T(8,128)(2,1)}) custom-call(s32[6]{0:T(128)S(1)} %reshape.182.range_ref, f32[384,512]{1,0:T(8,128)S(1)} %get-tuple-element.76.dy_ref, f32[384,512]{1,0:T(8,128)S(1)} %get-tuple-element.70.xin_ref.xhat_ref, ...), custom_call_target="tpu_custom_call" | custom-call | tf_op jit(solution)/shard_map/cross_backward/pallas_call | solution.py:501
  386.2 10.5 %self_backward.3 = (f32[640,512]{1,0:T(8,128)S(1)}, f32[2,512]{1,0:T(2,128)S(1)}, bf16[4,512,512]{2,1,0:T(8,128)(2,1)S(1)}) custom-call(f32[384,512]{1,0:T(8,128)S(1)} %copy-done.31, f32[384,512]{1,0:T(8,128)S(1)} %get-tuple-element.69.xin_ref.xhat_ref, f32[384,1]{1,0:T(8,128)S(1)} %copy-done.57, f32[2,512]{1,0:T(2,128)S(1)} %get-tuple-element.163.norm_ref.norm_in_ref, ...), custom_call_target="tpu_custom_call" | custom-call | tf_op jit(solution)/shard_map/self_backward/pallas_call | solution.py:269
  400.0 4.4 reduce-scatter.15.cloned.1.call-done.dy_ref
  410.5 5.9 feed_backward.3
  418.4 9.6 self_backward.2
  433.5 5.0 reduce-scatter.25.cloned.1.call-done
  438.6 33.9 %reduce-scatter.21.cloned.1.call-done = bf16[1,512,512]{2,1,0:T(8,128)(2,1)} async-done(((bf16[4,512,512]{2,1,0:T(8,128)(2,1)}), bf16[1,512,512]{2,1,0:T(8,128)(2,1)}) %reduce-scatter.21.cloned.1.call-update) | async-done | bytes 524304 | tf_op jit(solution)/shard_map/reduce_scatter | solution.py:660
  472.6 33.9 %reduce-scatter.17.cloned.1.call-done = bf16[1,512,512]{2,1,0:T(8,128)(2,1)} async-done(((bf16[4,512,512]{2,1,0:T(8,128)(2,1)}), bf16[1,512,512]{2,1,0:T(8,128)(2,1)}) %reduce-scatter.17.cloned.1.call-update) | async-done | bytes 524304 | tf_op jit(solution)/shard_map/reduce_scatter | solution.py:660
  511.7 41.9 %reduce-scatter.33.cloned.1.call-done = bf16[1,512,1024]{2,1,0:T(8,128)(2,1)} async-done(((bf16[4,512,1024]{2,1,0:T(8,128)(2,1)}), bf16[1,512,1024]{2,1,0:T(8,128)(2,1)}) %reduce-scatter.33.cloned.1.call-update) | async-done | bytes 1048592 | tf_op jit(solution)/shard_map/reduce_scatter | solution.py:660
  560.2 58.8 %reduce-scatter.37.cloned.1.call-done = f32[64,10]{1,0:T(8,128)} async-done(((f32[512,10]{1,0:T(8,128)}), f32[64,10]{1,0:T(8,128)}) %reduce-scatter.37.cloned.1.call-update) | async-done | bytes 2576
  620.0 6.0 psum.16
  629.3 54.5 %reduce-scatter.27.cloned.1.call-done = bf16[64,512]{1,0:T(8,128)(2,1)} async-done(((bf16[512,512]{1,0:T(8,128)(2,1)}), bf16[64,512]{1,0:T(8,128)(2,1)}) %reduce-scatter.27.cloned.1.call-update) | async-done | bytes 65552 | tf_op jit(solution)/shard_map/reduce_scatter | solution.py:661
  684.6 63.3 %reduce-scatter.23.cloned.1.call-done = bf16[64,512]{1,0:T(8,128)(2,1)} async-done(((bf16[512,512]{1,0:T(8,128)(2,1)}), bf16[64,512]{1,0:T(8,128)(2,1)}) %reduce-scatter.23.cloned.1.call-update) | async-done | bytes 65552 | tf_op jit(solution)/shard_map/reduce_scatter | solution.py:661
  751.7 60.6 %reduce-scatter.19.cloned.1.call-done = bf16[64,512]{1,0:T(8,128)(2,1)} async-done(((bf16[512,512]{1,0:T(8,128)(2,1)}), bf16[64,512]{1,0:T(8,128)(2,1)}) %reduce-scatter.19.cloned.1.call-update) | async-done | bytes 65552 | tf_op jit(solution)/shard_map/reduce_scatter | solution.py:661
  816.7 41.6 %reduce-scatter.29.cloned.1.call-done = bf16[1,512,1024]{2,1,0:T(8,128)(2,1)} async-done(((bf16[4,512,1024]{2,1,0:T(8,128)(2,1)}), bf16[1,512,1024]{2,1,0:T(8,128)(2,1)}) %reduce-scatter.29.cloned.1.call-update) | async-done | bytes 1048592 | tf_op jit(solution)/shard_map/reduce_scatter | solution.py:660
  858.5 67.0 %reduce-scatter.35.cloned.1.call-done = bf16[64,1024]{1,0:T(8,128)(2,1)} async-done(((bf16[512,1024]{1,0:T(8,128)(2,1)}), bf16[64,1024]{1,0:T(8,128)(2,1)}) %reduce-scatter.35.cloned.1.call-update) | async-done | bytes 131088 | tf_op jit(solution)/shard_map/reduce_scatter | solution.py:661
  928.0 63.2 %reduce-scatter.31.cloned.1.call-done = bf16[64,1024]{1,0:T(8,128)(2,1)} async-done(((bf16[512,1024]{1,0:T(8,128)(2,1)}), bf16[64,1024]{1,0:T(8,128)(2,1)}) %reduce-scatter.31.cloned.1.call-update) | async-done | bytes 131088 | tf_op jit(solution)/shard_map/reduce_scatter | solution.py:661
  995.1 40.0 %psum.15 = f32[]{:T(128)} all-reduce(f32[]{:T(128)S(6)} %add.193), channel_id=1, replica_groups=mesh['z'=4,'x'=2,'y'=2,'c'=2] {'z','x','y','c'}, use_global_device_ids=true, to_apply=%region_21.22 | all-reduce | flops 1 | bytes 8 | tf_op jit(solution)/shard_map/psum | solution.py:791
  (311 shorter events, 105.7 us)
Async XLA Ops:
  7.2 64.1 %all-gather.7.cloned.1.call-start = ((), (), s32[]{:S(2)}) async-start(), calls=%async_computation.12 | async-start | bytes 2162688 | tf_op jit(solution)/shard_map/all_gather | solution.py:654
  10.0 125.9 %all-gather.9.cloned.1.call-start = ((), (), s32[]{:S(2)}) async-start(), calls=%async_computation.13 | async-start | bytes 4325376 | tf_op jit(solution)/shard_map/all_gather | solution.py:654
  11.7 182.9 %all-gather.11.cloned.1.call-start = ((), (), s32[]{:S(2)}) async-start(), calls=%async_computation.14 | async-start | bytes 2162688 | tf_op jit(solution)/shard_map/all_gather | solution.py:654
  12.5 240.9 %all-gather.15.cloned.1.call-start = ((), (), s32[]{:S(2)}) async-start(), calls=%async_computation.16 | async-start | bytes 2162688 | tf_op jit(solution)/shard_map/all_gather | solution.py:654
  13.2 260.7 %all-gather.13.cloned.1.call-start = ((), (), s32[]{:S(2)}) async-start(), calls=%async_computation.15 | async-start | bytes 1966080 | tf_op jit(solution)/shard_map/all_gather | solution.py:750
  13.3 38.0 %collective-permute-start.1 = (bf16[128,512]{1,0:T(8,128)(2,1)S(1)}, bf16[128,512]{1,0:T(8,128)(2,1)S(1)}, u32[]{:S(2)}, u32[]{:S(2)}) collective-permute-start(bf16[128,512]{1,0:T(8,128)(2,1)S(1)} %get-tuple-element.139), channel_id=1, source_target_pairs={{1,0},{2,1},{3,2},{5,4},{6,5},{7,6},{9,8},{10,9},{11,10},{13,12},{... | collective-permute-start | bytes 393224 | tf_op jit(solution)/shard_map/ppermute | solution.py:667
  14.6 36.6 %collective-permute-start = (bf16[128,512]{1,0:T(8,128)(2,1)S(1)}, bf16[128,512]{1,0:T(8,128)(2,1)S(1)}, u32[]{:S(2)}, u32[]{:S(2)}) collective-permute-start(bf16[128,512]{1,0:T(8,128)(2,1)S(1)} %get-tuple-element.140), channel_id=1, source_target_pairs={{0,1},{1,2},{2,3},{4,5},{5,6},{6,7},{8,9},{9,10},{10,11},{12,13},{... | collective-permute-start | bytes 393224 | tf_op jit(solution)/shard_map/ppermute | solution.py:667
  147.3 192.2 %all-gather.17.cloned.1.call-start = ((), (), s32[]{:S(2)}) async-start(), calls=%async_computation.17 | async-start | bytes 4325376 | tf_op jit(solution)/shard_map/all_gather | solution.py:654
  148.0 256.4 %reduce-scatter.15.cloned.1.call-start = ((), (), s32[]{:S(2)}) async-start(), calls=%async_computation.18 | async-start | bytes 1966080 | tf_op jit(solution)/shard_map/reduce_scatter | solution.py:767
  148.3 4.9 collective-permute-start.2
  150.5 4.1 collective-permute-start.3
  376.6 61.9 %reduce-scatter.25.cloned.1.call-start = ((), (), s32[]{:S(2)}) async-start(), calls=%async_computation.23 | async-start | bytes 2621440 | tf_op jit(solution)/shard_map/reduce_scatter | solution.py:660
  377.4 95.2 %reduce-scatter.21.cloned.1.call-start = ((), (), s32[]{:S(2)}) async-start(), calls=%async_computation.21 | async-start | bytes 2621440 | tf_op jit(solution)/shard_map/reduce_scatter | solution.py:660
  399.8 106.8 %reduce-scatter.17.cloned.1.call-start = ((), (), s32[]{:S(2)}) async-start(), calls=%async_computation.19 | async-start | bytes 2621440 | tf_op jit(solution)/shard_map/reduce_scatter | solution.py:660
  428.0 125.6 %reduce-scatter.33.cloned.1.call-start = ((), (), s32[]{:S(2)}) async-start(), calls=%async_computation.27 | async-start | bytes 5242880 | tf_op jit(solution)/shard_map/reduce_scatter | solution.py:660
  428.8 190.2 %reduce-scatter.37.cloned.1.call-start = ((), (), s32[]{:S(2)}) async-start(), calls=%async_computation.29 | async-start | bytes 294912
  433.5 250.2 %reduce-scatter.27.cloned.1.call-start = ((), (), s32[]{:S(2)}) async-start(), calls=%async_computation.24 | async-start | bytes 589824 | tf_op jit(solution)/shard_map/reduce_scatter | solution.py:661
  438.6 309.3 %reduce-scatter.23.cloned.1.call-start = ((), (), s32[]{:S(2)}) async-start(), calls=%async_computation.22 | async-start | bytes 589824 | tf_op jit(solution)/shard_map/reduce_scatter | solution.py:661
  472.6 339.8 %reduce-scatter.19.cloned.1.call-start = ((), (), s32[]{:S(2)}) async-start(), calls=%async_computation.20 | async-start | bytes 589824 | tf_op jit(solution)/shard_map/reduce_scatter | solution.py:661
  506.5 351.7 %reduce-scatter.29.cloned.1.call-start = ((), (), s32[]{:S(2)}) async-start(), calls=%async_computation.25 | async-start | bytes 5242880 | tf_op jit(solution)/shard_map/reduce_scatter | solution.py:660
  507.1 418.4 %reduce-scatter.35.cloned.1.call-start = ((), (), s32[]{:S(2)}) async-start(), calls=%async_computation.28 | async-start | bytes 1179648 | tf_op jit(solution)/shard_map/reduce_scatter | solution.py:661
  507.9 50.2 %collective-permute-start.6 = (f32[128,512]{1,0:T(8,128)S(1)}, f32[128,512]{1,0:T(8,128)}, u32[]{:S(2)}, u32[]{:S(2)}) collective-permute-start(f32[128,512]{1,0:T(8,128)S(1)} %get-tuple-element.133), channel_id=1, source_target_pairs={{0,1},{1,2},{2,3},{4,5},{5,6},{6,7},{8,9},{9,10},{10,11},{12,13},{... | collective-permute-start | bytes 786440 | tf_op jit(solution)/shard_map/ppermute | solution.py:667
  510.4 47.8 %collective-permute-start.7 = (f32[128,512]{1,0:T(8,128)S(1)}, f32[128,512]{1,0:T(8,128)}, u32[]{:S(2)}, u32[]{:S(2)}) collective-permute-start(f32[128,512]{1,0:T(8,128)S(1)} %get-tuple-element.134), channel_id=1, source_target_pairs={{1,0},{2,1},{3,2},{5,4},{6,5},{7,6},{9,8},{10,9},{11,10},{13,12},{... | collective-permute-start | bytes 786440 | tf_op jit(solution)/shard_map/ppermute | solution.py:667
  553.6 437.6 %reduce-scatter.31.cloned.1.call-start = ((), (), s32[]{:S(2)}) async-start(), calls=%async_computation.26 | async-start | bytes 1179648 | tf_op jit(solution)/shard_map/reduce_scatter | solution.py:661
  554.4 72.8 %collective-permute-start.4 = (f32[128,512]{1,0:T(8,128)}, f32[128,512]{1,0:T(8,128)}, u32[]{:S(2)}, u32[]{:S(2)}) collective-permute-start(f32[128,512]{1,0:T(8,128)} %get-tuple-element.135), channel_id=1, source_target_pairs={{0,1},{1,2},{2,3},{4,5},{5,6},{6,7},{8,9},{9,10},{10,11},{12,13},{... | collective-permute-start | bytes 786440 | tf_op jit(solution)/shard_map/ppermute | solution.py:667
  556.9 70.4 %collective-permute-start.5 = (f32[128,512]{1,0:T(8,128)S(1)}, f32[128,512]{1,0:T(8,128)}, u32[]{:S(2)}, u32[]{:S(2)}) collective-permute-start(f32[128,512]{1,0:T(8,128)S(1)} %get-tuple-element.136), channel_id=1, source_target_pairs={{1,0},{2,1},{3,2},{5,4},{6,5},{7,6},{9,8},{10,9},{11,10},{13,12},{... | collective-permute-start | bytes 786440 | tf_op jit(solution)/shard_map/ppermute | solution.py:667
  858.3 177.5 %copy-start.82 = (f32[5,2,64]{2,1,0:T(2,128)S(1)}, f32[5,2,64]{2,1,0:T(2,128)}, u32[]{:S(2)}) copy-start(f32[5,2,64]{2,1,0:T(2,128)} %param.33) | copy-start | bytes 7684
  858.3 177.5 %copy-start.84 = (f32[5,2,64]{2,1,0:T(2,128)S(1)}, f32[5,2,64]{2,1,0:T(2,128)}, u32[]{:S(2)}) copy-start(f32[5,2,64]{2,1,0:T(2,128)} %param.38) | copy-start | bytes 7684
  858.3 177.5 %copy-start.85 = (f32[5,2,64]{2,1,0:T(2,128)S(1)}, f32[5,2,64]{2,1,0:T(2,128)}, u32[]{:S(2)}) copy-start(f32[5,2,64]{2,1,0:T(2,128)} %param.43) | copy-start | bytes 7684
  858.3 178.2 %copy-start.64 = (f32[9,64,128]{2,1,0:T(8,128)S(1)}, f32[9,64,128]{2,1,0:T(8,128)}, u32[]{:S(2)}) copy-start(f32[9,64,128]{2,1,0:T(8,128)} %param.29) | copy-start | bytes 884740
  858.3 178.1 %copy-start.72 = (f32[9,64,128]{2,1,0:T(8,128)S(1)}, f32[9,64,128]{2,1,0:T(8,128)}, u32[]{:S(2)}) copy-start(f32[9,64,128]{2,1,0:T(8,128)} %param.34) | copy-start | bytes 884740
  858.4 178.1 %copy-start.73 = (f32[9,64,128]{2,1,0:T(8,128)S(1)}, f32[9,64,128]{2,1,0:T(8,128)}, u32[]{:S(2)}) copy-start(f32[9,64,128]{2,1,0:T(8,128)} %param.39) | copy-start | bytes 884740
  (81 other events, 705.8 us)
Sparse Core Ops, SparseCore 0:
  11.6 59.6 all-gather.6
  74.9 60.9 all-gather.8
  139.4 55.1 all-gather.10
  198.0 55.3 all-gather.14
  255.4 18.5 all-gather.12
  277.3 62.0 all-gather.16
  376.7 27.6 reduce-scatter.14
  407.1 31.4 reduce-scatter.24
  441.1 31.4 reduce-scatter.20
  475.1 31.3 reduce-scatter.16
  509.0 44.5 reduce-scatter.32
  557.7 61.2 reduce-scatter.36
  622.7 60.9 reduce-scatter.26
  686.9 60.9 reduce-scatter.22
  751.4 60.8 reduce-scatter.18
  814.7 43.4 reduce-scatter.28
  861.9 63.5 reduce-scatter.34
  928.7 62.4 reduce-scatter.30

commit v2 on v1

v2 whole, which is shorter than its diff:
```python
import functools

import jax
import jax.numpy as jnp
from jax import lax
from jax.experimental import pallas as pl
from jax.experimental.pallas import tpu as pltpu
from jax.sharding import Mesh
from jax.sharding import PartitionSpec as P

HEAD_DIM = 64
STEP = 10
BLOCK = 128
PAIR = 2 * HEAD_DIM

norm_eps = 1e-05
beta_one = 0.9
beta_two = 0.98
adam_eps = 1e-08
weight_decay = 0.01
rate_matrix = 0.1
rate_norm = 0.5
clip_bound = 1.0
masked_score = -1e30
score_scale = HEAD_DIM ** (-0.5)
gelu_a = 0.7978845608028654
gelu_b = 0.044715

F32 = jnp.float32
BF16 = jnp.bfloat16
ANY = pl.ANY
SMEM = pltpu.SMEM
VMEM = pltpu.VMEM

NN = (((1,), (0,)), ((), ()))
NT = (((1,), (1,)), ((), ()))


def mm(a, b, dims=NN):
    return lax.dot_general(a, b, dims, preferred_element_type=F32)


def vmem(count):
    return [pl.BlockSpec(memory_space=VMEM)] * count


def smem(count):
    return [pl.BlockSpec(memory_space=SMEM)] * count


def hbm(count):
    return [pl.BlockSpec(memory_space=ANY)] * count


def params(mib=60):
    return pltpu.CompilerParams(vmem_limit_bytes=mib * 1024 * 1024)


def shaped(shape, dtype):
    return jax.ShapeDtypeStruct(shape, dtype)


def normalize(total):
    centred = total - jnp.mean(total, axis=-1, keepdims=True)
    spread = jnp.mean(centred * centred, axis=-1, keepdims=True)
    rstd = lax.rsqrt(spread + norm_eps)
    return centred * rstd, rstd


def norm_backward(grad_out, xhat, rstd, gain):
    scaled = grad_out * gain
    first = jnp.mean(scaled, axis=-1, keepdims=True)
    second = jnp.mean(scaled * xhat, axis=-1, keepdims=True)
    return rstd * (scaled - first - xhat * second)


def norm_param_grads(grad_out, xhat):
    return (
        jnp.sum(grad_out * xhat, axis=0, keepdims=True),
        jnp.sum(grad_out, axis=0, keepdims=True),
    )


def half_masks():
    lane = lax.broadcasted_iota(jnp.int32, (1, PAIR), 1)
    low = jnp.where(lane < HEAD_DIM, 1.0, 0.0).astype(BF16)
    high = jnp.where(lane < HEAD_DIM, 0.0, 1.0).astype(BF16)
    return low, high


def stack_pair(values, masks):
    return jnp.concatenate([values * masks[0], values * masks[1]], axis=0)


SLAB = 64


def slots(member):
    side, row = member % 2, member // 2
    return [(side, (2 * row + x) * 4 + z, 2 * z + x) for x in range(2) for z in range(4)]


def slab_rows(me_ref, block):
    return pl.ds(pl.multiple_of((me_ref[0] ^ block) * SLAB, SLAB), SLAB)


def weight_copies(me_ref, pieces, offset, w_vmem, sems):
    width = w_vmem.shape[2]
    copies = []
    for member in range(4):
        copies.append(
            [
                pltpu.make_async_copy(
                    pieces[side].at[slot, :, pl.ds(offset, width)],
                    w_vmem.at[member, slab_rows(me_ref, block), :],
                    sems.at[member, block],
                )
                for side, slot, block in slots(member)
            ]
        )
    return copies


def grad_copies(me_ref, dw_vmem, pieces, offset, sems):
    width = dw_vmem.shape[2]
    copies = []
    for member in range(4):
        copies.append(
            [
                pltpu.make_async_copy(
                    dw_vmem.at[member, slab_rows(me_ref, block), :],
                    pieces[side].at[slot, :, pl.ds(offset, width)],
                    sems.at[member, block],
                )
                for side, slot, block in slots(member)
            ]
        )
    return copies


def start_all(groups):
    for group in groups:
        for copy in group:
            copy.start()


def wait_all(group):
    for copy in group:
        copy.wait()


def spread_kinds(w_vmem, w_flat, member):
    part = w_vmem.shape[2] // 4
    for kind in range(4):
        w_flat[:, pl.ds((kind * 4 + member) * part, part)] = w_vmem[
            member, :, kind * part : (kind + 1) * part
        ]


def store_kind(dw_vmem, kind, grads):
    part = dw_vmem.shape[2] // 4
    for member in range(4):
        dw_vmem[member, :, kind * part : (kind + 1) * part] = grads[
            :, member * part : (member + 1) * part
        ].astype(BF16)


def self_forward_kernel(
    offset, me_ref, x_ref, segq_ref, segk_ref, own_hbm, sib_hbm,
    xhat_ref, rstd_ref, q_ref, k_ref, v_ref, ctx_ref, pt_ref,
    w_vmem, w_s, vt_s, ctxt_s, sems,
):
    copies = weight_copies(me_ref, (own_hbm, sib_hbm), offset, w_vmem, sems)
    start_all(copies)
    rows, width = q_ref.shape
    blocks, pairs = rows // BLOCK, width // PAIR
    window = 3 * BLOCK
    for member in range(4):
        wait_all(copies[member])
        spread_kinds(w_vmem, w_s, member)
    kv = mm(x_ref[...], w_s[:, width : 3 * width]).astype(BF16)
    k_ref[...] = kv[:, :width]
    v_ref[...] = kv[:, width:]
    vt_s[...] = kv[:, width:].T
    q = mm(x_ref[BLOCK : BLOCK + rows, :], w_s[:, :width]).astype(BF16)
    q_ref[...] = q * jnp.asarray(score_scale, BF16)
    masks = half_masks()
    for block in range(blocks):
        at = pl.ds(block * BLOCK, BLOCK)
        keys_at = pl.ds(block * BLOCK, window)
        allowed = segk_ref[keys_at, :] == segq_ref[block : block + 1, :]
        for pair in range(pairs):
            cols = pl.ds(pair * PAIR, PAIR)
            stacked = stack_pair(q_ref[at, cols], masks)
            scores = mm(k_ref[keys_at, cols], stacked, NT)
            scores = jnp.where(allowed, scores, masked_score)
            highest = jnp.max(scores, axis=0, keepdims=True)
            raised = jnp.exp(scores - highest)
            total = jnp.sum(raised, axis=0, keepdims=True)
            probs = (raised * (1.0 / total)).astype(BF16)
            pt_ref[block * pairs + pair] = probs
            context = mm(vt_s[cols, keys_at], probs).astype(BF16)
            ctxt_s[pl.ds(pair * PAIR, HEAD_DIM), at] = context[:HEAD_DIM, :BLOCK]
            ctxt_s[pl.ds(pair * PAIR + HEAD_DIM, HEAD_DIM), at] = context[HEAD_DIM:, BLOCK:]
    context = ctxt_s[...].T
    ctx_ref[...] = context
    branch = mm(context, w_s[:, 3 * width :], NT)
    xhat, rstd = normalize(x_ref[BLOCK : BLOCK + rows, :].astype(F32) + branch)
    xhat_ref[...] = xhat
    rstd_ref[...] = rstd


def self_forward(me, x, segq, segk, weights):
    (own, sib), offset = weights
    keys, width = x.shape
    rows = keys - 2 * BLOCK
    blocks, pairs = rows // BLOCK, width // PAIR
    return pl.pallas_call(
        functools.partial(self_forward_kernel, offset),
        out_shape=(
            shaped((rows, width), F32),
            shaped((rows, 1), F32),
            shaped((rows, width), BF16),
            shaped((keys, width), BF16),
            shaped((keys, width), BF16),
            shaped((rows, width), BF16),
            shaped((blocks * pairs, 3 * BLOCK, 2 * BLOCK), BF16),
        ),
        in_specs=smem(1) + vmem(3) + hbm(2),
        out_specs=tuple(vmem(7)),
        scratch_shapes=[
            pltpu.VMEM((4, width, width), BF16),
            pltpu.VMEM((width, 4 * width), BF16),
            pltpu.VMEM((width, keys), BF16),
            pltpu.VMEM((width, rows), BF16),
            pltpu.SemaphoreType.DMA((4, width // SLAB)),
        ],
        compiler_params=params(),
        name="self_forward",
    )(me, x, segq, segk, own, sib)


def self_backward_kernel(
    offset, out_offset, k_norm, prior, me_ref, dy_ref, xhat_ref, rstd_ref, norms_ref, x_ref,
    q_ref, k_ref, v_ref, ctx_ref, pt_ref, own_hbm, sib_hbm, *rest,
):
    rest = rest[prior:]
    dx_ref, before_ref, after_ref, dnorm_ref, keep_hbm, send_hbm = rest[:6]
    w_vmem, w_s, dw_s, dctx_s, kt_s, dqt_s, dkv_s, sems, out_sems = rest[6:]
    copies = weight_copies(me_ref, (own_hbm, sib_hbm), offset, w_vmem, sems)
    start_all(copies)
    out_copies = grad_copies(me_ref, dw_s, (keep_hbm, send_hbm), out_offset, out_sems)
    rows, width = q_ref.shape
    blocks, pairs = rows // BLOCK, width // PAIR
    window = 3 * BLOCK
    masks = half_masks()
    dy = dy_ref[...]
    xhat = xhat_ref[...]
    dgain, dshift = norm_param_grads(dy, xhat)
    dnorm_ref[0:1, :] = dgain
    dnorm_ref[1:2, :] = dshift
    dtotal = norm_backward(dy, xhat, rstd_ref[...], norms_ref[2 * k_norm : 2 * k_norm + 1, :])
    low = dtotal.astype(BF16)
    for member in range(4):
        wait_all(copies[member])
        spread_kinds(w_vmem, w_s, member)
    dctx_s[...] = mm(low, w_s[:, 3 * width :]).astype(BF16)
    store_kind(dw_s, 3, mm(low.T, ctx_ref[...]))
    kt_s[...] = k_ref[...].T
    dkv_s[...] = jnp.zeros_like(dkv_s)
    for block in range(blocks):
        at = pl.ds(block * BLOCK, BLOCK)
        keys_at = pl.ds(block * BLOCK, window)
        for pair in range(pairs):
            cols = pl.ds(pair * PAIR, PAIR)
            dstacked = stack_pair(dctx_s[at, cols], masks)
            qstacked = stack_pair(q_ref[at, cols], masks)
            probs_low = pt_ref[block * pairs + pair]
            probs = probs_low.astype(F32)
            dprobs = mm(v_ref[keys_at, cols], dstacked, NT)
            delta = jnp.sum(probs * dprobs, axis=0, keepdims=True)
            dscores = (probs * (dprobs - delta)).astype(BF16)
            dkv_s[keys_at, cols] += mm(dscores, qstacked)
            dkv_s[keys_at, pl.ds(width + pair * PAIR, PAIR)] += mm(probs_low, dstacked)
            dqt = mm(kt_s[cols, keys_at], dscores) * score_scale
            dqt = dqt.astype(BF16)
            dqt_s[pl.ds(pair * PAIR, HEAD_DIM), at] = dqt[:HEAD_DIM, :BLOCK]
            dqt_s[pl.ds(pair * PAIR + HEAD_DIM, HEAD_DIM), at] = dqt[HEAD_DIM:, BLOCK:]
    dq = dqt_s[...].T
    dkv = dkv_s[...].astype(BF16)
    xt = x_ref[...].T
    store_kind(dw_s, 0, mm(xt[:, BLOCK : BLOCK + rows], dq))
    store_kind(dw_s, 1, mm(xt, dkv[:, :width]))
    store_kind(dw_s, 2, mm(xt, dkv[:, width:]))
    start_all(out_copies)
    dx = mm(dkv, w_s[:, width : 3 * width], NT)
    before_ref[...] = dx[:BLOCK]
    after_ref[...] = dx[BLOCK + rows :]
    dx_ref[...] = dx[BLOCK : BLOCK + rows] + dtotal + mm(dq, w_s[:, :width], NT)
    for group in out_copies:
        wait_all(group)


def self_backward(me, dy, xhat, rstd, norms, k_norm, x, saved, weights, grads):
    (own, sib), offset = weights
    prior, out_offset, out_width = grads
    keys, width = x.shape
    rows = keys - 2 * BLOCK
    piece = shaped((16, SLAB, out_width), BF16)
    return pl.pallas_call(
        functools.partial(self_backward_kernel, offset, out_offset, k_norm, len(prior)),
        out_shape=(
            shaped((rows, width), F32),
            shaped((BLOCK, width), F32),
            shaped((BLOCK, width), F32),
            shaped((2, width), F32),
            piece,
            piece,
        ),
        in_specs=smem(1) + vmem(10) + hbm(2 + len(prior)),
        out_specs=(*vmem(4), *hbm(2)),
        input_output_aliases={13 + i: 4 + i for i in range(len(prior))},
        scratch_shapes=[
            pltpu.VMEM((4, width, width), BF16),
            pltpu.VMEM((width, 4 * width), BF16),
            pltpu.VMEM((4, width, width), BF16),
            pltpu.VMEM((rows, width), BF16),
            pltpu.VMEM((width, keys), BF16),
            pltpu.VMEM((width, rows), BF16),
            pltpu.VMEM((keys, 2 * width), F32),
            pltpu.SemaphoreType.DMA((4, width // SLAB)),
            pltpu.SemaphoreType.DMA((4, width // SLAB)),
        ],
        compiler_params=params(),
        name="self_backward",
    )(me, dy, xhat, rstd, norms, x, *saved, own, sib, *prior)


def memory_copies(me_ref, pieces, m_s, sems):
    rows = pieces[0].shape[0]
    return [
        pltpu.make_async_copy(
            piece,
            m_s.at[pl.ds(pl.multiple_of((me_ref[1] ^ member) * rows, rows), rows), :],
            sems.at[member],
        )
        for member, piece in enumerate(pieces)
    ]


def cross_forward_kernel(
    offset, k_in, me_ref, range_ref, xin_ref, norms_ref, segq_ref, segk_ref,
    m0_hbm, m1_hbm, m2_hbm, m3_hbm, own_hbm, sib_hbm,
    xhat_ref, rstd_ref, q_ref, k_ref, v_ref, ctx_ref, lse_ref,
    m_s, w_vmem, w_s, vt_s, s_s, acc_s, ctxt_s, sems, m_sems,
):
    copies = weight_copies(me_ref, (own_hbm, sib_hbm), offset, w_vmem, sems)
    start_all(copies)
    m_copies = memory_copies(me_ref, (m0_hbm, m1_hbm, m2_hbm, m3_hbm), m_s, m_sems)
    start_all([m_copies])
    rows, width = q_ref.shape
    blocks, pairs = rows // BLOCK, width // PAIR
    masks = half_masks()
    gain, shift = norms_ref[2 * k_in : 2 * k_in + 1, :], norms_ref[2 * k_in + 1 : 2 * k_in + 2, :]
    inputs = xin_ref[...] * gain + shift
    for member in range(4):
        wait_all(copies[member])
        spread_kinds(w_vmem, w_s, member)
    q = mm(inputs.astype(BF16), w_s[:, :width]).astype(BF16)
    q_ref[...] = q * jnp.asarray(score_scale, BF16)
    wait_all(m_copies)

    @pl.loop(range_ref[0], range_ref[2 * blocks - 1])
    def _(key_block):
        keys_at = pl.ds(pl.multiple_of(key_block * BLOCK, BLOCK), BLOCK)
        kv = mm(m_s[keys_at, :], w_s[:, width : 3 * width]).astype(BF16)
        k_ref[keys_at, :] = kv[:, :width]
        v_ref[keys_at, :] = kv[:, width:]
        vt_s[:, keys_at] = kv[:, width:].T

    for block in range(blocks):
        at = pl.ds(block * BLOCK, BLOCK)
        first, last = range_ref[2 * block], range_ref[2 * block + 1]
        stacked = [stack_pair(q_ref[at, pl.ds(p * PAIR, PAIR)], masks) for p in range(pairs)]
        segq = segq_ref[block : block + 1, :]

        def scan_scores(key_block, highest):
            keys_at = pl.ds(pl.multiple_of(key_block * BLOCK, BLOCK), BLOCK)
            allowed = segk_ref[keys_at, :] == segq
            result = []
            for pair in range(pairs):
                scores = mm(k_ref[keys_at, pl.ds(pair * PAIR, PAIR)], stacked[pair], NT)
                scores = jnp.where(allowed, scores, masked_score)
                s_s[pair, keys_at, :] = scores
                result.append(
                    jnp.maximum(highest[pair], jnp.max(scores, axis=0, keepdims=True))
                )
            return tuple(result)

        start = tuple(jnp.full((1, 2 * BLOCK), masked_score, F32) for _ in range(pairs))
        highest = lax.fori_loop(first, last, scan_scores, start)
        acc_s[...] = jnp.zeros_like(acc_s)

        def scan_context(key_block, sums):
            keys_at = pl.ds(pl.multiple_of(key_block * BLOCK, BLOCK), BLOCK)
            result = []
            for pair in range(pairs):
                raised = jnp.exp(s_s[pair, keys_at, :] - highest[pair])
                result.append(sums[pair] + jnp.sum(raised, axis=0, keepdims=True))
                acc_s[pair] += mm(vt_s[pl.ds(pair * PAIR, PAIR), keys_at], raised.astype(BF16))
            return tuple(result)

        start = tuple(jnp.zeros((1, 2 * BLOCK), F32) for _ in range(pairs))
        sums = lax.fori_loop(first, last, scan_context, start)
        for pair in range(pairs):
            context = (acc_s[pair] * (1.0 / sums[pair])).astype(BF16)
            ctxt_s[pl.ds(pair * PAIR, HEAD_DIM), at] = context[:HEAD_DIM, :BLOCK]
            ctxt_s[pl.ds(pair * PAIR + HEAD_DIM, HEAD_DIM), at] = context[HEAD_DIM:, BLOCK:]
            row = block * pairs + pair
            lse_ref[row : row + 1, :] = highest[pair] + jnp.log(sums[pair])
    context = ctxt_s[...].T
    ctx_ref[...] = context
    branch = mm(context, w_s[:, 3 * width :], NT)
    xhat, rstd = normalize(inputs + branch)
    xhat_ref[...] = xhat
    rstd_ref[...] = rstd


def cross_forward(me, ranges, xin, norms, k_in, segq, segk, memory, weights):
    (own, sib), offset = weights
    rows, width = xin.shape
    keys = 4 * rows
    blocks, pairs = rows // BLOCK, width // PAIR
    return pl.pallas_call(
        functools.partial(cross_forward_kernel, offset, k_in),
        out_shape=(
            shaped((rows, width), F32),
            shaped((rows, 1), F32),
            shaped((rows, width), BF16),
            shaped((keys, width), BF16),
            shaped((keys, width), BF16),
            shaped((rows, width), BF16),
            shaped((blocks * pairs, 2 * BLOCK), F32),
        ),
        in_specs=smem(2) + vmem(4) + hbm(6),
        out_specs=tuple(vmem(7)),
        scratch_shapes=[
            pltpu.VMEM((keys, width), BF16),
            pltpu.VMEM((4, width, width), BF16),
            pltpu.VMEM((width, 4 * width), BF16),
            pltpu.VMEM((width, keys), BF16),
            pltpu.VMEM((pairs, keys, 2 * BLOCK), F32),
            pltpu.VMEM((pairs, PAIR, 2 * BLOCK), F32),
            pltpu.VMEM((width, rows), BF16),
            pltpu.SemaphoreType.DMA((4, width // SLAB)),
            pltpu.SemaphoreType.DMA((4,)),
        ],
        compiler_params=params(),
        name="cross_forward",
    )(me, ranges, xin, norms, segq, segk, *memory, own, sib)


def cross_backward_kernel(
    offset, out_offset, k_norm, k_in, prior, me_ref, range_ref, dy_ref, xhat_ref, rstd_ref,
    norms_ref, xin_ref, segq_ref, segk_ref, q_ref, k_ref, v_ref, ctx_ref, lse_ref,
    m0_hbm, m1_hbm, m2_hbm, m3_hbm, own_hbm, sib_hbm, *rest,
):
    rest = rest[prior:]
    dx_ref, dnorm_ref, dm_keep, dm_send, keep_hbm, send_hbm = rest[:6]
    (
        m_s, w_vmem, w_s, dw_s, dctx_s, kt_s, dqt_acc, dqt_s, dkv_s, dwkv_s, dm_s,
        sems, out_sems, m_sems, dm_sems,
    ) = rest[6:]
    copies = weight_copies(me_ref, (own_hbm, sib_hbm), offset, w_vmem, sems)
    start_all(copies)
    m_copies = memory_copies(me_ref, (m0_hbm, m1_hbm, m2_hbm, m3_hbm), m_s, m_sems)
    start_all([m_copies])
    out_copies = grad_copies(me_ref, dw_s, (keep_hbm, send_hbm), out_offset, out_sems)
    rows, width = q_ref.shape
    blocks, pairs = rows // BLOCK, width // PAIR
    heads_here = width // HEAD_DIM
    masks = half_masks()
    dy = dy_ref[...]
    xhat = xhat_ref[...]
    dgain, dshift = norm_param_grads(dy, xhat)
    dnorm_ref[0:1, :] = dgain
    dnorm_ref[1:2, :] = dshift
    dtotal = norm_backward(dy, xhat, rstd_ref[...], norms_ref[2 * k_norm : 2 * k_norm + 1, :])
    low = dtotal.astype(BF16)
    for member in range(4):
        wait_all(copies[member])
        spread_kinds(w_vmem, w_s, member)
    dctx = mm(low, w_s[:, 3 * width :]).astype(BF16)
    dctx_s[...] = dctx
    store_kind(dw_s, 3, mm(low.T, ctx_ref[...]))
    products = (dctx.astype(F32) * ctx_ref[...].astype(F32)).T
    deltas = [
        jnp.sum(products[h * HEAD_DIM : (h + 1) * HEAD_DIM, :], axis=0, keepdims=True)
        for h in range(heads_here)
    ]
    everything_first, everything_last = range_ref[0], range_ref[2 * blocks - 1]

    @pl.loop(everything_first, everything_last)
    def _(key_block):
        keys_at = pl.ds(pl.multiple_of(key_block * BLOCK, BLOCK), BLOCK)
        kt_s[:, keys_at] = k_ref[keys_at, :].T
        dkv_s[keys_at, :] = jnp.zeros((BLOCK, 2 * width), F32)

    for block in range(blocks):
        at = pl.ds(block * BLOCK, BLOCK)
        lanes = slice(block * BLOCK, (block + 1) * BLOCK)
        first, last = range_ref[2 * block], range_ref[2 * block + 1]
        qstacked = [stack_pair(q_ref[at, pl.ds(p * PAIR, PAIR)], masks) for p in range(pairs)]
        dstacked = [stack_pair(dctx_s[at, pl.ds(p * PAIR, PAIR)], masks) for p in range(pairs)]
        delta = [
            jnp.concatenate([deltas[2 * p][:, lanes], deltas[2 * p + 1][:, lanes]], axis=1)
            for p in range(pairs)
        ]
        segq = segq_ref[block : block + 1, :]
        dqt_acc[...] = jnp.zeros_like(dqt_acc)

        @pl.loop(first, last)
        def _(key_block):
            keys_at = pl.ds(pl.multiple_of(key_block * BLOCK, BLOCK), BLOCK)
            allowed = segk_ref[keys_at, :] == segq
            for pair in range(pairs):
                cols = pl.ds(pair * PAIR, PAIR)
                row = block * pairs + pair
                scores = mm(k_ref[keys_at, cols], qstacked[pair], NT)
                scores = jnp.where(allowed, scores, masked_score)
                probs = jnp.exp(scores - lse_ref[row : row + 1, :])
                dprobs = mm(v_ref[keys_at, cols], dstacked[pair], NT)
                dscores = (probs * (dprobs - delta[pair])).astype(BF16)
                dkv_s[keys_at, cols] += mm(dscores, qstacked[pair])
                dkv_s[keys_at, pl.ds(width + pair * PAIR, PAIR)] += mm(
                    probs.astype(BF16), dstacked[pair]
                )
                dqt_acc[pair] += mm(kt_s[cols, keys_at], dscores)

        for pair in range(pairs):
            dqt = (dqt_acc[pair] * score_scale).astype(BF16)
            dqt_s[pl.ds(pair * PAIR, HEAD_DIM), at] = dqt[:HEAD_DIM, :BLOCK]
            dqt_s[pl.ds(pair * PAIR + HEAD_DIM, HEAD_DIM), at] = dqt[HEAD_DIM:, BLOCK:]
    dq = dqt_s[...].T
    gain, shift = norms_ref[2 * k_in : 2 * k_in + 1, :], norms_ref[2 * k_in + 1 : 2 * k_in + 2, :]
    inputs = (xin_ref[...] * gain + shift).astype(BF16)
    store_kind(dw_s, 0, mm(inputs.T, dq))
    dx_ref[...] = dtotal + mm(dq, w_s[:, :width], NT)
    dm_s[...] = jnp.zeros_like(dm_s)
    dwkv_s[...] = jnp.zeros_like(dwkv_s)
    wait_all(m_copies)

    @pl.loop(everything_first, everything_last)
    def _(key_block):
        keys_at = pl.ds(pl.multiple_of(key_block * BLOCK, BLOCK), BLOCK)
        dkv = dkv_s[keys_at, :].astype(BF16)
        dm_s[keys_at, :] = mm(dkv, w_s[:, width : 3 * width], NT).astype(BF16)
        dwkv_s[...] += mm(m_s[keys_at, :].T, dkv)

    dm_copies = [
        pltpu.make_async_copy(
            dm_s.at[pl.ds(pl.multiple_of((me_ref[1] ^ member) * rows, rows), rows), :],
            (dm_keep, dm_send)[member % 2].at[member // 2],
            dm_sems.at[member],
        )
        for member in range(4)
    ]
    start_all([dm_copies])
    store_kind(dw_s, 1, dwkv_s[:, :width])
    store_kind(dw_s, 2, dwkv_s[:, width:])
    start_all(out_copies)
    wait_all(dm_copies)
    for group in out_copies:
        wait_all(group)


def cross_backward(
    me, ranges, dy, xhat, rstd, norms, k_norm, xin, k_in, segq, segk, saved, memory, weights, grads
):
    (own, sib), offset = weights
    prior, out_offset, out_width = grads
    rows, width = xin.shape
    keys = 4 * rows
    pairs = width // PAIR
    piece = shaped((16, SLAB, out_width), BF16)
    half = shaped((2, rows, width), BF16)
    return pl.pallas_call(
        functools.partial(cross_backward_kernel, offset, out_offset, k_norm, k_in, len(prior)),
        out_shape=(shaped((rows, width), F32), shaped((2, width), F32), half, half, piece, piece),
        in_specs=smem(2) + vmem(12) + hbm(6 + len(prior)),
        out_specs=(*vmem(2), *hbm(4)),
        input_output_aliases={20 + i: 4 + i for i in range(len(prior))},
        scratch_shapes=[
            pltpu.VMEM((keys, width), BF16),
            pltpu.VMEM((4, width, width), BF16),
            pltpu.VMEM((width, 4 * width), BF16),
            pltpu.VMEM((4, width, width), BF16),
            pltpu.VMEM((rows, width), BF16),
            pltpu.VMEM((width, keys), BF16),
            pltpu.VMEM((pairs, PAIR, 2 * BLOCK), F32),
            pltpu.VMEM((width, rows), BF16),
            pltpu.VMEM((keys, 2 * width), F32),
            pltpu.VMEM((width, 2 * width), F32),
            pltpu.VMEM((keys, width), BF16),
            pltpu.SemaphoreType.DMA((4, width // SLAB)),
            pltpu.SemaphoreType.DMA((4, width // SLAB)),
            pltpu.SemaphoreType.DMA((4,)),
            pltpu.SemaphoreType.DMA((4,)),
        ],
        compiler_params=params(),
        name="cross_backward",
    )(me, ranges, dy, xhat, rstd, norms, xin, segq, segk, *saved, *memory, own, sib, *prior)


def gelu_and_slope(pre):
    square = pre * pre
    tanh = jnp.tanh(gelu_a * pre * (1.0 + gelu_b * square))
    cdf = 0.5 + 0.5 * tanh
    slope = cdf + (0.5 * gelu_a) * pre * (1.0 - tanh * tanh) * (1.0 + (3.0 * gelu_b) * square)
    return (pre * cdf).astype(BF16), slope.astype(BF16)


def feed_members_forward(low, acc_s, w_vmem, copies, hidden_ref, slope_ref):
    half = w_vmem.shape[2] // 2
    for member in range(4):
        wait_all(copies[member])
        hidden, slope = gelu_and_slope(mm(low, w_vmem[member, :, :half]))
        hidden_ref[member] = hidden
        slope_ref[member] = slope
        acc_s[...] += mm(hidden, w_vmem[member, :, half:], NT)


def feed_members_backward(
    low, x_low, dx_ref, w_vmem, copies, hidden_ref, slope_ref, dw_s, out_copies
):
    half = w_vmem.shape[2] // 2
    lowt = low.T
    xt = x_low.T
    for member in range(4):
        if copies is not None:
            wait_all(copies[member])
        dhidden = mm(low, w_vmem[member, :, half:])
        dpre = (dhidden * slope_ref[member].astype(F32)).astype(BF16)
        dw_s[member, :, :half] = mm(xt, dpre).astype(BF16)
        dw_s[member, :, half:] = mm(lowt, hidden_ref[member]).astype(BF16)
        start_all([out_copies[member]])
        dx_ref[...] += mm(dpre, w_vmem[member, :, :half], NT)
    for group in out_copies:
        wait_all(group)


def feed_forward_kernel(
    offset, norm_offset, k_in, k_out, me_ref, xin_ref, own_hbm, sib_hbm, norm_own_hbm,
    xhat_ref, rstd_ref, out_ref, hidden_ref, slope_ref, norms_ref,
    w_vmem, norm_s, acc_s, sems, norm_sems,
):
    copies = weight_copies(me_ref, (own_hbm, sib_hbm), offset, w_vmem, sems)
    norm_copies = [
        pltpu.make_async_copy(
            norm_own_hbm.at[slot, :, pl.ds(norm_offset, BLOCK)],
            norm_s.at[slab_rows(me_ref, block), :],
            norm_sems.at[block],
        )
        for side, slot, block in slots(0)
    ]
    start_all([norm_copies] + copies)
    wait_all(norm_copies)
    norms = norm_s[...].astype(F32).T[: norms_ref.shape[0], :]
    norms_ref[...] = norms
    inputs = xin_ref[...] * norms[2 * k_in : 2 * k_in + 1] + norms[2 * k_in + 1 : 2 * k_in + 2]
    acc_s[...] = inputs
    feed_members_forward(inputs.astype(BF16), acc_s, w_vmem, copies, hidden_ref, slope_ref)
    xhat, rstd = normalize(acc_s[...])
    xhat_ref[...] = xhat
    rstd_ref[...] = rstd
    normed = xhat * norms[2 * k_out : 2 * k_out + 1] + norms[2 * k_out + 1 : 2 * k_out + 2]
    out_ref[...] = normed.astype(BF16)


def feed_forward(me, xin, k_in, k_out, weights, norm_piece):
    (own, sib), offset = weights
    (norm_own, _), norm_offset = norm_piece
    rows, width = xin.shape
    part = shaped((4, rows, width), BF16)
    return pl.pallas_call(
        functools.partial(feed_forward_kernel, offset, norm_offset, k_in, k_out),
        out_shape=(
            shaped((rows, width), F32),
            shaped((rows, 1), F32),
            shaped((rows, width), BF16),
            part,
            part,
            shaped((16, width), F32),
        ),
        in_specs=smem(1) + vmem(1) + hbm(3),
        out_specs=tuple(vmem(6)),
        scratch_shapes=[
            pltpu.VMEM((4, width, 2 * width), BF16),
            pltpu.VMEM((width, BLOCK), BF16),
            pltpu.VMEM((rows, width), F32),
            pltpu.SemaphoreType.DMA((4, width // SLAB)),
            pltpu.SemaphoreType.DMA((width // SLAB,)),
        ],
        compiler_params=params(),
        name="feed_forward",
    )(me, xin, own, sib, norm_own)


def feed_backward_kernel(
    offset, out_offset, k_in, k_out, prior, me_ref, dy_ref, xhat_ref, rstd_ref, norms_ref, xin_ref,
    hidden_ref, slope_ref, own_hbm, sib_hbm, *rest,
):
    rest = rest[prior:]
    dx_ref, dnorm_ref, keep_hbm, send_hbm, w_vmem, dw_s, sems, out_sems = rest
    copies = weight_copies(me_ref, (own_hbm, sib_hbm), offset, w_vmem, sems)
    start_all(copies)
    out_copies = grad_copies(me_ref, dw_s, (keep_hbm, send_hbm), out_offset, out_sems)
    dy = dy_ref[...].astype(F32)
    xhat = xhat_ref[...]
    dgain, dshift = norm_param_grads(dy, xhat)
    dnorm_ref[0:1, :] = dgain
    dnorm_ref[1:2, :] = dshift
    dtotal = norm_backward(dy, xhat, rstd_ref[...], norms_ref[2 * k_out : 2 * k_out + 1, :])
    dx_ref[...] = dtotal
    gain, shift = norms_ref[2 * k_in : 2 * k_in + 1, :], norms_ref[2 * k_in + 1 : 2 * k_in + 2, :]
    inputs = (xin_ref[...] * gain + shift).astype(BF16)
    feed_members_backward(
        dtotal.astype(BF16), inputs, dx_ref, w_vmem, copies, hidden_ref, slope_ref, dw_s, out_copies
    )


def feed_backward(me, dy, xhat, rstd, norms, xin, k_in, k_out, hidden, slope, weights, grads):
    (own, sib), offset = weights
    prior, out_offset, out_width = grads
    rows, width = xin.shape
    piece = shaped((16, SLAB, out_width), BF16)
    return pl.pallas_call(
        functools.partial(feed_backward_kernel, offset, out_offset, k_in, k_out, len(prior)),
        out_shape=(shaped((rows, width), F32), shaped((2, width), F32), piece, piece),
        in_specs=smem(1) + vmem(7) + hbm(2 + len(prior)),
        out_specs=(*vmem(2), *hbm(2)),
        input_output_aliases={10 + i: 2 + i for i in range(len(prior))},
        scratch_shapes=[
            pltpu.VMEM((4, width, 2 * width), BF16),
            pltpu.VMEM((4, width, 2 * width), BF16),
            pltpu.SemaphoreType.DMA((4, width // SLAB)),
            pltpu.SemaphoreType.DMA((4, width // SLAB)),
        ],
        compiler_params=params(),
        name="feed_backward",
    )(me, dy, xhat, rstd, norms, xin, hidden, slope, own, sib, *prior)


def feed_turn_kernel(
    offset, out_offset, k_in, k_out, me_ref, xin_ref, norms_ref, dy_ref, own_hbm, sib_hbm,
    out_ref, dx_ref, dnorm_ref, keep_hbm, send_hbm,
    w_vmem, dw_s, hidden_s, slope_s, sems, out_sems,
):
    copies = weight_copies(me_ref, (own_hbm, sib_hbm), offset, w_vmem, sems)
    start_all(copies)
    out_copies = grad_copies(me_ref, dw_s, (keep_hbm, send_hbm), out_offset, out_sems)
    gain, shift = norms_ref[2 * k_in : 2 * k_in + 1, :], norms_ref[2 * k_in + 1 : 2 * k_in + 2, :]
    inputs = xin_ref[...] * gain + shift
    dx_ref[...] = inputs
    low = inputs.astype(BF16)
    feed_members_forward(low, dx_ref, w_vmem, copies, hidden_s, slope_s)
    xhat, rstd = normalize(dx_ref[...])
    gain = norms_ref[2 * k_out : 2 * k_out + 1, :]
    out_ref[...] = (xhat * gain + norms_ref[2 * k_out + 1 : 2 * k_out + 2, :]).astype(BF16)
    dy = dy_ref[...].astype(F32)
    dgain, dshift = norm_param_grads(dy, xhat)
    dnorm_ref[0:1, :] = dgain
    dnorm_ref[1:2, :] = dshift
    dtotal = norm_backward(dy, xhat, rstd, gain)
    dx_ref[...] = dtotal
    feed_members_backward(
        dtotal.astype(BF16), low, dx_ref, w_vmem, None, hidden_s, slope_s, dw_s, out_copies
    )


def feed_turn(me, xin, norms, k_in, k_out, dy, weights, grads):
    (own, sib), offset = weights
    _, out_offset, out_width = grads
    rows, width = xin.shape
    piece = shaped((16, SLAB, out_width), BF16)
    return pl.pallas_call(
        functools.partial(feed_turn_kernel, offset, out_offset, k_in, k_out),
        out_shape=(
            shaped((rows, width), BF16),
            shaped((rows, width), F32),
            shaped((2, width), F32),
            piece,
            piece,
        ),
        in_specs=smem(1) + vmem(3) + hbm(2),
        out_specs=(*vmem(3), *hbm(2)),
        scratch_shapes=[
            pltpu.VMEM((4, width, 2 * width), BF16),
            pltpu.VMEM((4, width, 2 * width), BF16),
            pltpu.VMEM((4, rows, width), BF16),
            pltpu.VMEM((4, rows, width), BF16),
            pltpu.SemaphoreType.DMA((4, width // SLAB)),
            pltpu.SemaphoreType.DMA((4, width // SLAB)),
        ],
        compiler_params=params(),
        name="feed_turn",
    )(me, xin, norms, dy, own, sib)


DP = ("z", "x")
MP = ("y", "c")
ALL = ("z", "x", "y", "c")


def is_cube():
    return tuple(lax.axis_size(axis) for axis in ALL) == (4, 2, 2, 2)


def swap(values, axis, distance=1):
    return lax.ppermute(values, axis, [(i, i ^ distance) for i in range(lax.axis_size(axis))])


def gather_pieces(shard):
    if not is_cube():
        whole = lax.all_gather(shard, MP + DP, axis=0, tiled=True)
        whole = whole.reshape(2, 2, 4, 2, SLAB, shard.shape[1])
        whole = whole.transpose(1, 0, 3, 2, 4, 5)
        whole = whole.reshape(2, 16, SLAB, shard.shape[1])
        return whole[0], whole[1]
    lines = jnp.stack([shard] + [swap(shard, "z", k) for k in (1, 2, 3)])
    over_x, over_y = swap(lines, "x"), swap(lines, "y")
    far_one, far_two = swap(over_y[:2], "x"), swap(over_x[2:], "y")
    own = jnp.concatenate([lines, over_x, over_y, far_one, far_two], axis=0)
    return own, swap(own, "c")


def add(*terms):
    return sum(term.astype(F32) for term in terms)


def reduce_pieces(keep, send):
    if not is_cube():
        whole = jnp.stack([keep, send]).reshape(2, 2, 2, 4, SLAB, keep.shape[2])
        whole = whole.transpose(1, 0, 3, 2, 4, 5).reshape(4, 8 * SLAB, keep.shape[2])
        part = lax.psum_scatter(whole, MP, scatter_dimension=0, tiled=True)
        part = lax.psum_scatter(part[0], DP, scatter_dimension=0, tiled=True)
        return part.astype(F32)
    got = swap(send, "c")
    far_one = swap(add(keep[12:14], got[12:14]).astype(BF16), "x")
    far_two = swap(add(keep[14:16], got[14:16]).astype(BF16), "y")
    to_x = jnp.concatenate(
        [add(keep[4:6], got[4:6]).astype(BF16), add(keep[6:8], got[6:8], far_two).astype(BF16)]
    )
    to_y = jnp.concatenate(
        [add(keep[8:10], got[8:10], far_one).astype(BF16), add(keep[10:12], got[10:12]).astype(BF16)]
    )
    from_x, from_y = swap(to_x, "x"), swap(to_y, "y")
    lines = [
        add(keep[k], got[k], from_x[k], from_y[k]).astype(F32 if k == 0 else BF16) for k in range(4)
    ]
    return add(lines[0], *(swap(lines[k], "z", k) for k in (1, 2, 3)))


def sum_all(values):
    if not is_cube():
        return lax.psum(values, ALL)
    for axis, distance in (("c", 1), ("y", 1), ("x", 1), ("z", 1), ("z", 2)):
        values = values + swap(values, axis, distance)
    return values


def gather_memory(values):
    if not is_cube():
        whole = lax.all_gather(values, MP, axis=0, tiled=False)
        return tuple(whole[k] for k in range(4))
    over_y, over_c = swap(values, "y"), swap(values, "c")
    return (values, over_c, over_y, swap(over_y, "c"))


def reduce_memory(keep, send):
    if not is_cube():
        whole = jnp.stack([keep[0], send[0], keep[1], send[1]])
        return lax.psum_scatter(whole, MP, scatter_dimension=0, tiled=True)[0].astype(F32)
    got = swap(send, "c")
    over_y = swap(add(keep[1], got[1]).astype(BF16), "y")
    return add(keep[0], got[0], over_y)


def shift_rows(values, step):
    count = lax.axis_size(MP)
    pairs = [(i, i + step) for i in range(count) if 0 <= i + step < count]
    return lax.ppermute(values, MP, pairs)


def with_halos(first, second):
    before = shift_rows(jnp.concatenate([first[-BLOCK:], second[-BLOCK:]]), 1)
    after = shift_rows(jnp.concatenate([first[:BLOCK], second[:BLOCK]]), -1)
    return (
        jnp.concatenate([before[:BLOCK], first, after[:BLOCK]]),
        jnp.concatenate([before[BLOCK:], second, after[BLOCK:]]),
    )


def add_halos(values, before, after):
    rows = values.shape[0]
    return (
        values
        + jnp.pad(before, ((0, rows - BLOCK), (0, 0)))
        + jnp.pad(after, ((rows - BLOCK, 0), (0, 0)))
    )


def adam_step(weights, first, second, grads, rate, decay):
    first_new = beta_one * first + (1.0 - beta_one) * grads
    second_new = beta_two * second + (1.0 - beta_two) * grads * grads
    first_hat = first_new / (1.0 - beta_one**STEP)
    second_hat = second_new / (1.0 - beta_two**STEP)
    weights_new = weights - rate * (first_hat / (jnp.sqrt(second_hat) + adam_eps) + decay * weights)
    return (weights_new, first_new, second_new)


GATHERS = (("enc",), ("enc_feed", "norms", "self"), ("cross",), ("dec_feed",))
REDUCES = (("dec_feed",), ("cross", "self"), ("enc_feed",), ("enc",))


def on_device(
    encoder_input, decoder_copy, decoder_target, decoder_cotangent,
    source_segments, target_segments, glance_mask,
    attention_in, attention_out, feed_in, feed_out, norm_params,
    attention_in_first, attention_out_first, feed_in_first, feed_out_first, norm_params_first,
    attention_in_second, attention_out_second, feed_in_second, feed_out_second, norm_params_second,
):
    rows, width = encoder_input.shape
    part, half = attention_in.shape[2], feed_in.shape[2]
    masters = (attention_in, attention_out, feed_in, feed_out, norm_params)

    def attention_shard(number):
        kinds = [attention_in[3 * number + kind] for kind in range(3)]
        return jnp.concatenate(kinds + [attention_out[number].T], axis=1)

    def feed_shard(number):
        return jnp.concatenate([feed_in[number], feed_out[number].T], axis=1)

    norm_columns = norm_params.reshape(10, -1).T
    shards = {
        "enc": attention_shard(0),
        "enc_feed": feed_shard(0),
        "norms": jnp.pad(norm_columns, ((0, 0), (0, BLOCK - 10))),
        "self": attention_shard(1),
        "cross": attention_shard(2),
        "dec_feed": feed_shard(1),
    }
    weights = {}
    for group in GATHERS:
        joined = jnp.concatenate([shards[name].astype(BF16) for name in group], axis=1)
        pieces = gather_pieces(joined)
        offset = 0
        for name in group:
            weights[name] = (pieces, offset)
            offset += shards[name].shape[1]

    picked = glance_mask[0] == 1
    decoder_input = jnp.where(picked[:, None], decoder_target, decoder_copy)
    encoder_x, decoder_x = with_halos(encoder_input, decoder_input)

    member = lax.axis_index(MP)
    position = member * rows
    blocks = rows // BLOCK
    me = jnp.stack([lax.axis_index(DP), member]) if is_cube() else jnp.zeros((2,), jnp.int32)
    me = me.astype(jnp.int32)

    def query_segments(row):
        own = lax.dynamic_slice(row, (position,), (rows,)).reshape(blocks, BLOCK)
        return jnp.concatenate([own, own], axis=1)

    def key_segments(row):
        padded = jnp.pad(row, (BLOCK, BLOCK), constant_values=-1)
        return lax.dynamic_slice(padded, (position,), (rows + 2 * BLOCK,))[:, None]

    source_row, target_row = source_segments[0], target_segments[0]
    source_q, target_q = query_segments(source_row), query_segments(target_row)
    source_k, target_k = key_segments(source_row), key_segments(target_row)
    lowest, highest = target_q[:, 0], target_q[:, BLOCK - 1]
    first_key = jnp.sum((source_row[None, :] < lowest[:, None]).astype(jnp.int32), axis=1)
    last_key = jnp.sum((source_row[None, :] <= highest[:, None]).astype(jnp.int32), axis=1)
    ranges = jnp.stack([first_key // BLOCK, (last_key + BLOCK - 1) // BLOCK], axis=1)
    ranges = ranges.astype(jnp.int32).reshape(2 * blocks)
    source_column = source_row[:, None]

    grads, buffers = {}, {}
    for group in REDUCES:
        offset = 0
        total = sum(shards[name].shape[1] for name in group)
        for name in group:
            grads[name] = (group, offset, total)
            offset += shards[name].shape[1]

    def target(name):
        group, offset, total = grads[name]
        return (buffers.get(group, ()), offset, total)

    def keep_grads(name, pieces):
        buffers[grads[name][0]] = tuple(pieces)

    reduced_groups = {}

    def finish(name):
        group = grads[name][0]
        reduced_groups[group] = reduce_pieces(*buffers[group])

    xhat0, rstd0, *enc_saved = self_forward(me, encoder_x, source_q, source_k, weights["enc"])
    xhat1, rstd1, encoder_output, enc_hidden, enc_slope, norms = feed_forward(
        me, xhat0, 0, 1, weights["enc_feed"], weights["norms"]
    )
    memory = gather_memory(encoder_output)
    xhat2, rstd2, *self_saved = self_forward(me, decoder_x, target_q, target_k, weights["self"])
    xhat3, rstd3, *cross_saved = cross_forward(
        me, ranges, xhat2, norms, 2, target_q, source_column, memory, weights["cross"]
    )
    decoder_output, d4, dnorm4, *pieces = feed_turn(
        me, xhat3, norms, 3, 4, decoder_cotangent, weights["dec_feed"], target("dec_feed")
    )
    keep_grads("dec_feed", pieces)
    finish("dec_feed")

    d3, dnorm3, dm_keep, dm_send, *pieces = cross_backward(
        me, ranges, d4, xhat3, rstd3, norms, 3, xhat2, 2, target_q, source_column, cross_saved,
        memory, weights["cross"], target("cross"),
    )
    keep_grads("cross", pieces)
    dmemory = reduce_memory(dm_keep, dm_send)
    dx_dec, before_dec, after_dec, dnorm2, *pieces = self_backward(
        me, d3, xhat2, rstd2, norms, 2, decoder_x, self_saved, weights["self"], target("self")
    )
    keep_grads("self", pieces)
    finish("self")
    d1, dnorm1, *pieces = feed_backward(
        me, dmemory, xhat1, rstd1, norms, xhat0, 0, 1, enc_hidden, enc_slope,
        weights["enc_feed"], target("enc_feed"),
    )
    keep_grads("enc_feed", pieces)
    finish("enc_feed")
    dx_enc, before_enc, after_enc, dnorm0, *pieces = self_backward(
        me, d1, xhat0, rstd0, norms, 0, encoder_x, enc_saved, weights["enc"], target("enc")
    )
    keep_grads("enc", pieces)
    finish("enc")
    before = shift_rows(jnp.concatenate([after_enc, after_dec]), 1)
    after = shift_rows(jnp.concatenate([before_enc, before_dec]), -1)
    encoder_input_grad = add_halos(dx_enc, before[:BLOCK], after[:BLOCK])
    decoder_input_grad = add_halos(dx_dec, before[BLOCK:], after[BLOCK:])

    reduced = {}
    for group, values in reduced_groups.items():
        for name in group:
            offset = grads[name][1]
            reduced[name] = values[:, offset : offset + shards[name].shape[1]]
    squares = sum(jnp.sum(values * values) for values in reduced_groups.values())
    payload = jnp.concatenate(
        [dnorm0, dnorm1, dnorm2, dnorm3, dnorm4, jnp.broadcast_to(squares, (1, width))]
    )
    payload = sum_all(payload)
    g_all = payload[:10]
    grad_norm = jnp.sqrt(payload[10, 0] + jnp.sum(g_all * g_all))
    factor = clip_bound / jnp.maximum(grad_norm, clip_bound)
    own_columns = norm_params.shape[2]
    g_norms = lax.dynamic_slice(g_all, (0, lax.axis_index(DP) * own_columns), (10, own_columns))

    attention_parts = [reduced[name] for name in ("enc", "self", "cross")]
    feed_parts = [reduced[name] for name in ("enc_feed", "dec_feed")]
    g_in = jnp.stack(
        [g[:, kind * part : (kind + 1) * part] for g in attention_parts for kind in range(3)]
    )
    g_out = jnp.stack([g[:, 3 * part :].T for g in attention_parts])
    g_first = jnp.stack([g[:, :half] for g in feed_parts])
    g_second = jnp.stack([g[:, half:].T for g in feed_parts])
    all_grads = (g_in, g_out, g_first, g_second, g_norms.reshape(norm_params.shape))
    firsts = (
        attention_in_first, attention_out_first, feed_in_first, feed_out_first, norm_params_first,
    )
    seconds = (
        attention_in_second, attention_out_second, feed_in_second, feed_out_second,
        norm_params_second,
    )
    results = []
    for number in range(5):
        rate = rate_norm if number == 4 else rate_matrix
        decay = 0.0 if number == 4 else weight_decay
        results.append(
            adam_step(
                masters[number],
                firsts[number],
                seconds[number],
                all_grads[number] * factor,
                rate,
                decay,
            )
        )
    return (
        encoder_output,
        decoder_output,
        encoder_input_grad,
        decoder_input_grad,
        grad_norm,
        *(result[0] for result in results),
        *(result[1] for result in results),
        *(result[2] for result in results),
    )


def solution(mesh):
    dp, mp = mesh.shape["dp"], mesh.shape["mp"]
    fine = Mesh(mesh.devices.reshape(dp // 2, 2, mp // 2, 2), ALL)
    tokens = P(ALL, None)
    columns = P(None, DP, MP)
    turned = P(None, MP, DP)
    states = (columns, turned, columns, turned, P(None, None, DP))
    return jax.shard_map(
        on_device,
        mesh=fine,
        in_specs=(
            *((tokens,) * 4),
            P(DP, None),
            P(DP, None),
            P(DP, MP),
            *states,
            *states,
            *states,
        ),
        out_specs=(*((tokens,) * 4), P(), *states, *states, *states),
        check_vma=False,
    )
```

time: 1060 us -> 458 us (0.43)
  waiting for transfers between devices: 756 us -> 143 us
  blocking collectives: 78.9 us -> 0 us
  starting transfers between devices: 16.8 us -> 90.9 us
  Pallas kernels: 87.6 us -> 123 us
  other arithmetic: 27.8 us -> 47 us
  local copies, waits for them, and re-layouts: 60.6 us -> 43 us
  between operations: 21.3 us -> 7.28 us
    reduce_scatter x11 -> x0, waiting for transfers between devices: 469 us -> none  [the longest x5 309 us: scatter_grads(): return lax.psum_scatter(part[0], DP, scatter_dimension=0, tiled=True)]
    all_gather x6 -> x0, waiting for transfers between devices: 224 us -> none  [the longest x5 203 us: gather_weights(): gathered = lax.all_gather(shard, MP + DP, axis=0, tiled=True)]
    ppermute x0 -> x74, waiting for transfers between devices: none -> 143 us  [swap(): lax.ppermute(values, axis, [(i, i ^ distance) for i in range(lax.axis_siz...]
    ppermute x0 -> x74, starting transfers between devices: none -> 82.9 us  [swap(): lax.ppermute(values, axis, [(i, i ^ distance) for i in range(lax.axis_siz...]
    unnamed x19 -> x0, waiting for transfers between devices: 61 us -> none
    psum x2 -> x0, blocking collectives: 46 us -> none  [the longest x1 40 us: on_device(): grad_norm = jnp.sqrt(lax.psum(squares, ALL))]
    unnamed x192 -> x139, local copies, waits for them, and re-layouts: 58.3 us -> 22.7 us
    pallas_call x10 -> x9, Pallas kernels: 87.6 us -> 123 us  [the longest x2 29.4 us: self_backward(): pl.pallas_call(functools.partial(self_backward_kernel, offset, out_offset...]
  transfers between devices with their start and end apart: 26 -> 78, of which waited for: 19 -> 38; matrix products, arithmetic and copies ran while one was open for 3% -> 15% of each run, Pallas kernels for 5% -> 19%
where the time goes in v2:
time: 458 us; the launch traced here: 454 us
  waiting for transfers between devices  143 us (31%)
  Pallas kernels  123 us (27%)
  starting transfers between devices  90.9 us (20%)
  other arithmetic  47 us (10%)
  local copies, waits for them, and re-layouts  43 us (9%)
  between operations  7.28 us (2%)
    ppermute x74, waiting for transfers between devices, swap(): lax.ppermute(values, axis, [(i, i ^ distance) for i in range(lax.axis_siz...  143 us
    ppermute x74, starting transfers between devices, swap(): lax.ppermute(values, axis, [(i, i ^ distance) for i in range(lax.axis_siz...  82.9 us
    pallas_call x2, Pallas kernels, self_backward(): pl.pallas_call(functools.partial(self_backward_kernel, offset, out_offset...  29.4 us
    pallas_call x1, Pallas kernels, cross_backward(): pl.pallas_call(functools.partial(cross_backward_kernel, offset, out_offse...  23.5 us
    pallas_call x2, Pallas kernels, self_forward(): pl.pallas_call(functools.partial(self_forward_kernel, offset), out_shape=...  23.3 us
    unnamed x139, local copies, waits for them, and re-layouts  22.7 us
    pallas_call x1, Pallas kernels, cross_forward(): pl.pallas_call(functools.partial(cross_forward_kernel, offset, k_in), out...  13.2 us
    pallas_call x1, Pallas kernels, feed_turn(): pl.pallas_call(functools.partial(feed_turn_kernel, offset, out_offset, k_...  13.2 us
  transfers between devices with their start and end apart: 78, of which 38 were waited for; matrix products, arithmetic and copies ran while one was open for 15% of the time, Pallas kernels for 19%

profile of v2, /device:TPU:0, one launch (start us, length us, event | category | flops | bytes accessed | tf_op | source)
XLA Modules:
  0.0 453.9 jit_solution(4907163412572392347)
XLA Ops:
  3.6 5.0 %collective-permute-start.4 = (bf16[64,512]{1,0:T(8,128)(2,1)}, bf16[64,512]{1,0:T(8,128)(2,1)}, u32[]{:S(2)}, u32[]{:S(2)}) collective-permute-start(bf16[64,512]{1,0:T(8,128)(2,1)} %pad_maximum_fusion.19), channel_id=1, source_target_pairs={{0,24},{8,16},{16,8},{24,0},{1,25},{9,17},{17,9},{25,1},{2,26},{10... | collective-permute-start | bytes 196616 | tf_op jit(solution)/shard_map/ppermute | solution.py:820
  9.9 3.8 collective-permute-start.23
  36.1 3.8 collective-permute-start.12
  43.0 3.8 collective-permute-done.12
  49.9 10.3 %collective-permute-done.11 = bf16[64,1664]{1,0:T(8,128)(2,1)S(1)} collective-permute-done((bf16[64,1664]{1,0:T(8,128)(2,1)S(1)}, bf16[64,1664]{1,0:T(8,128)(2,1)S(1)}, u32[]{:S(2)}, u32[]{:S(2)}) %collective-permute-start.11) | collective-permute-done | bytes 213024 | tf_op jit(solution)/shard_map/ppermute | solution.py:820
  63.5 15.6 %collective-permute-done.14 = bf16[4,64,1664]{2,1,0:T(8,128)(2,1)S(1)} collective-permute-done((bf16[4,64,1664]{2,1,0:T(8,128)(2,1)S(1)}, bf16[4,64,1664]{2,1,0:T(8,128)(2,1)S(1)}, u32[]{:S(2)}, u32[]{:S(2)}) %collective-permute-start.14) | collective-permute-done | bytes 852000 | tf_op jit(solution)/shard_map/ppermute | solution.py:820
  82.6 6.9 %collective-permute-done.15 = bf16[2,64,1664]{2,1,0:T(8,128)(2,1)S(1)} collective-permute-done((bf16[2,64,1664]{2,1,0:T(8,128)(2,1)S(1)}, bf16[2,64,1664]{2,1,0:T(8,128)(2,1)S(1)}, u32[]{:S(2)}, u32[]{:S(2)}) %collective-permute-start.15) | collective-permute-done | bytes 426016 | tf_op jit(solution)/shard_map/ppermute | solution.py:820
  110.4 9.2 %collective-permute-done.33 = bf16[4,64,1024]{2,1,0:T(8,128)(2,1)S(1)} collective-permute-done((bf16[4,64,1024]{2,1,0:T(8,128)(2,1)S(1)}, bf16[4,64,1024]{2,1,0:T(8,128)(2,1)S(1)}, u32[]{:S(2)}, u32[]{:S(2)}) %collective-permute-start.33) | collective-permute-done | bytes 524320 | tf_op jit(solution)/shard_map/ppermute | solution.py:820
  124.3 8.6 %collective-permute-done.34 = bf16[2,64,1024]{2,1,0:T(8,128)(2,1)S(1)} collective-permute-done((bf16[2,64,1024]{2,1,0:T(8,128)(2,1)S(1)}, bf16[2,64,1024]{2,1,0:T(8,128)(2,1)S(1)}, u32[]{:S(2)}, u32[]{:S(2)}) %collective-permute-start.34) | collective-permute-done | bytes 262176 | tf_op jit(solution)/shard_map/ppermute | solution.py:820
  143.2 4.1 collective-permute-done.27
  149.6 11.5 %self_forward.2 = (f32[384,512]{1,0:T(8,128)}, f32[384,1]{1,0:T(8,128)}, bf16[384,512]{1,0:T(8,128)(2,1)}, bf16[640,512]{1,0:T(8,128)(2,1)}, bf16[640,512]{1,0:T...) custom-call(s32[2]{0:T(128)} %pad_add_fusion.5.me_ref, bf16[640,512]{1,0:T(8,128)(2,1)} %pad_maximum_fusion.1.x_ref, ...), custom_call_target="tpu_custom_call" | custom-call | tf_op jit(solution)/shard_map/self_forward/pallas_call | solution.py:218
  161.1 9.3 %feed_forward.1 = (f32[384,512]{1,0:T(8,128)}, f32[384,1]{1,0:T(8,128)}, bf16[384,512]{1,0:T(8,128)(2,1)}, bf16[4,384,512]{2,1,0:T(8,128)(2,1)}, bf16[4,384,512]{2,1,0:T(8,128)(2,1)}, /*index=5*/f32[16,512]{1,0:T(8,128)}) custom-call(s32[2]{0:T(128)} %pad_add_fusion.5.me_ref, f32[384,512]{1,0:T(8,128)} %get-tuple-element.74.xin_ref.xhat_ref, ...), custom_call_target="tpu_custom_call" | custom-call | tf_op jit(solution)/shard_map/feed_forward/pallas_call | solution.py:685
  173.0 9.3 %collective-permute-done.19.m2_hbm = bf16[384,512]{1,0:T(8,128)(2,1)S(1)} collective-permute-done((bf16[384,512]{1,0:T(8,128)(2,1)}, bf16[384,512]{1,0:T(8,128)(2,1)S(1)}, u32[]{:S(2)}, u32[]{:S(2)}) %collective-permute-start.19) | collective-permute-done | bytes 393248 | tf_op jit(solution)/shard_map/ppermute | solution.py:820
  186.7 11.9 %self_forward.3 = (f32[384,512]{1,0:T(8,128)}, f32[384,1]{1,0:T(8,128)}, bf16[384,512]{1,0:T(8,128)(2,1)}, bf16[640,512]{1,0:T(8,128)(2,1)}, bf16[640,512]{1,0:T...) custom-call(s32[2]{0:T(128)} %pad_add_fusion.5.me_ref, bf16[640,512]{1,0:T(8,128)(2,1)} %pad_maximum_fusion.2.x_ref, ...), custom_call_target="tpu_custom_call" | custom-call | tf_op jit(solution)/shard_map/self_forward/pallas_call | solution.py:218
  199.5 13.2 %cross_forward.1 = (f32[384,512]{1,0:T(8,128)}, f32[384,1]{1,0:T(8,128)}, bf16[384,512]{1,0:T(8,128)(2,1)}, bf16[1536,512]{1,0:T(8,128)(2,1)}, bf16[1536,512]{1,...) custom-call(s32[2]{0:T(128)} %pad_add_fusion.5.me_ref, s32[6]{0:T(128)} %reshape.432.range_ref, ...), custom_call_target="tpu_custom_call" | custom-call | tf_op jit(solution)/shard_map/cross_forward/pallas_call | solution.py:434
  212.8 13.2 %feed_turn.1 = (bf16[384,512]{1,0:T(8,128)(2,1)}, f32[384,512]{1,0:T(8,128)}, f32[2,512]{1,0:T(2,128)}, bf16[16,64,1024]{2,1,0:T(8,128)(2,1)}, bf16[16,64,1024]{2,1,0:T(8,128)(2,1)}) custom-call(s32[2]{0:T(128)} %pad_add_fusion.5.me_ref, f32[384,512]{1,0:T(8,128)} %get-tuple-element.78.xin_ref.xhat_ref, f32[16,512]{1,0:T(8,128)} %get-tuple-element.77.norms_ref, ...), custom_call_target="tpu_custom_call" | custom-call | tf_op jit(solution)/shard_map/feed_turn/pallas_call | solution.py:786
  226.0 23.5 %cross_backward.1 = (f32[384,512]{1,0:T(8,128)}, f32[2,512]{1,0:T(2,128)}, bf16[2,384,512]{2,1,0:T(8,128)(2,1)}, bf16[2,384,512]{2,1,0:T(8,128)(2,1)}, bf16[16,6...) custom-call(s32[2]{0:T(128)} %pad_add_fusion.5.me_ref, s32[6]{0:T(128)} %reshape.432.range_ref, ...), custom_call_target="tpu_custom_call" | custom-call | tf_op jit(solution)/shard_map/cross_backward/pallas_call | solution.py:587
  253.5 14.8 %self_backward.3 = (f32[384,512]{1,0:T(8,128)}, f32[128,512]{1,0:T(8,128)}, f32[128,512]{1,0:T(8,128)}, f32[2,512]{1,0:T(2,128)}, bf16[16,64,1024]{2,1,0:T(8,128)(2,1)}, /*index=5*/bf16[16,64,1024]{2,1,0:T(8,128)(2,1)}) custom-call(s32[2]{0:T(128)} %pad_add_fusion.5.me_ref, ...), custom_call_target="tpu_custom_call", output_to_operand_aliasing={{4}: (13, {}), {5}: (14, {})} | custom-call | tf_op jit(solution)/shard_map/self_backward/pallas_call | solution.py:310
  270.9 10.8 %feed_backward.1 = (f32[384,512]{1,0:T(8,128)}, f32[2,512]{1,0:T(2,128)}, bf16[16,64,1024]{2,1,0:T(8,128)(2,1)}, bf16[16,64,1024]{2,1,0:T(8,128)(2,1)}) custom-call(s32[2]{0:T(128)} %pad_add_fusion.5.me_ref, f32[384,512]{1,0:T(8,128)} %bitcast_add_fusion.dy_ref, f32[384,512]{1,0:T(8,128)} %get-tuple-element.89.xhat_ref, ...), custom_call_target="tpu_custom_call" | custom-call | tf_op jit(solution)/shard_map/feed_backward/pallas_call | solution.py:737
  281.7 14.6 %self_backward.2 = (f32[384,512]{1,0:T(8,128)}, f32[128,512]{1,0:T(8,128)}, f32[128,512]{1,0:T(8,128)}, f32[2,512]{1,0:T(2,128)}, bf16[16,64,512]{2,1,0:T(8,128)(2,1)}, /*index=5*/bf16[16,64,512]{2,1,0:T(8,128)(2,1)}) custom-call(s32[2]{0:T(128)} %pad_add_fusion.5.me_ref, f32[384,512]{1,0:T(8,128)} %get-tuple-element.93.dy_ref, ...), custom_call_target="tpu_custom_call" | custom-call | tf_op jit(solution)/shard_map/self_backward/pallas_call | solution.py:310
  301.3 3.3 collective-permute-start.39
  314.3 7.3 %collective-permute-start.52 = (bf16[2,64,1024]{2,1,0:T(8,128)(2,1)S(1)}, bf16[2,64,1024]{2,1,0:T(8,128)(2,1)S(1)}, u32[]{:S(2)}, u32[]{:S(2)}) collective-permute-start(bf16[2,64,1024]{2,1,0:T(8,128)(2,1)S(1)} %get-tuple-element.172), channel_id=1, source_target_pairs={{0,4},{4,0},{1,5},{5,1},{2,6},{6,2},{3,7},{7,3},{8,12},{12,8},{9,1... | collective-permute-start | bytes 786440 | tf_op jit(solution)/shard_map/ppermute | solution.py:820
  321.7 4.1 collective-permute-start.50
  326.6 5.1 %collective-permute-done.68 = bf16[2,64,512]{2,1,0:T(8,128)(2,1)S(1)} collective-permute-done((bf16[2,64,512]{2,1,0:T(8,128)(2,1)S(1)}, bf16[2,64,512]{2,1,0:T(8,128)(2,1)S(1)}, u32[]{:S(2)}, u32[]{:S(2)}) %collective-permute-start.68) | collective-permute-done | bytes 131104 | tf_op jit(solution)/shard_map/ppermute | solution.py:820
  343.9 5.2 %collective-permute-done.69 = bf16[4,64,512]{2,1,0:T(8,128)(2,1)S(1)} collective-permute-done((bf16[4,64,512]{2,1,0:T(8,128)(2,1)S(1)}, bf16[4,64,512]{2,1,0:T(8,128)(2,1)S(1)}, u32[]{:S(2)}, u32[]{:S(2)}) %collective-permute-start.69) | collective-permute-done | bytes 262176 | tf_op jit(solution)/shard_map/ppermute | solution.py:820
  349.4 3.4 collective-permute-start.71
  360.4 8.1 %collective-permute-done.51 = bf16[4,64,1024]{2,1,0:T(8,128)(2,1)S(1)} collective-permute-done((bf16[4,64,1024]{2,1,0:T(8,128)(2,1)S(1)}, bf16[4,64,1024]{2,1,0:T(8,128)(2,1)S(1)}, u32[]{:S(2)}, u32[]{:S(2)}) %collective-permute-start.51) | collective-permute-done | bytes 524320 | tf_op jit(solution)/shard_map/ppermute | solution.py:820
  381.7 6.7 %collective-permute-done.55 = bf16[64,1024]{1,0:T(8,128)(2,1)S(1)} collective-permute-done((bf16[64,1024]{1,0:T(8,128)(2,1)S(1)}, bf16[64,1024]{1,0:T(8,128)(2,1)S(1)}, u32[]{:S(2)}, u32[]{:S(2)}) %collective-permute-start.55) | collective-permute-done | bytes 131104 | tf_op jit(solution)/shard_map/ppermute | solution.py:820
  398.8 7.3 %collective-permute-done.61 = bf16[4,64,1024]{2,1,0:T(8,128)(2,1)} collective-permute-done((bf16[4,64,1024]{2,1,0:T(8,128)(2,1)S(1)}, bf16[4,64,1024]{2,1,0:T(8,128)(2,1)}, u32[]{:S(2)}, u32[]{:S(2)}) %collective-permute-start.61) | collective-permute-done | bytes 524320 | tf_op jit(solution)/shard_map/ppermute | solution.py:820
  412.3 3.7 collective-permute-done.62
  434.4 3.3 collective-permute-done.76
  437.7 4.7 %collective-permute-done.77 = f32[11,512]{1,0:T(8,128)S(1)} collective-permute-done((f32[11,512]{1,0:T(8,128)S(1)}, f32[11,512]{1,0:T(8,128)S(1)}, u32[]{:S(2)}, u32[]{:S(2)}) %collective-permute-start.77) | collective-permute-done | bytes 22560 | tf_op jit(solution)/shard_map/ppermute | solution.py:820
  (383 shorter events, 181.0 us)
Async XLA Ops:
  3.6 37.2 %collective-permute-start.4 = (bf16[64,512]{1,0:T(8,128)(2,1)}, bf16[64,512]{1,0:T(8,128)(2,1)}, u32[]{:S(2)}, u32[]{:S(2)}) collective-permute-start(bf16[64,512]{1,0:T(8,128)(2,1)} %pad_maximum_fusion.19), channel_id=1, source_target_pairs={{0,24},{8,16},{16,8},{24,0},{1,25},{9,17},{17,9},{25,1},{2,26},{10... | collective-permute-start | bytes 196616 | tf_op jit(solution)/shard_map/ppermute | solution.py:820
  8.7 27.5 %collective-permute-start.3 = (bf16[64,512]{1,0:T(8,128)(2,1)}, bf16[64,512]{1,0:T(8,128)(2,1)}, u32[]{:S(2)}, u32[]{:S(2)}) collective-permute-start(bf16[64,512]{1,0:T(8,128)(2,1)} %pad_maximum_fusion.19), channel_id=1, source_target_pairs={{0,16},{8,24},{16,0},{24,8},{1,17},{9,25},{17,1},{25,9},{2,18},{10... | collective-permute-start | bytes 196616 | tf_op jit(solution)/shard_map/ppermute | solution.py:820
  8.7 26.0 %collective-permute-start.2 = (bf16[64,512]{1,0:T(8,128)(2,1)}, bf16[64,512]{1,0:T(8,128)(2,1)}, u32[]{:S(2)}, u32[]{:S(2)}) collective-permute-start(bf16[64,512]{1,0:T(8,128)(2,1)} %pad_maximum_fusion.19), channel_id=1, source_target_pairs={{0,8},{8,0},{16,24},{24,16},{1,9},{9,1},{17,25},{25,17},{2,10},{10... | collective-permute-start | bytes 196616 | tf_op jit(solution)/shard_map/ppermute | solution.py:820
  9.9 84.4 %collective-permute-start.23 = (bf16[64,512]{1,0:T(8,128)(2,1)}, bf16[64,512]{1,0:T(8,128)(2,1)}, u32[]{:S(2)}, u32[]{:S(2)}) collective-permute-start(bf16[64,512]{1,0:T(8,128)(2,1)} %pad_maximum_fusion.20), channel_id=1, source_target_pairs={{0,24},{8,16},{16,8},{24,0},{1,25},{9,17},{17,9},{25,1},{2,26},{10... | collective-permute-start | bytes 196616 | tf_op jit(solution)/shard_map/ppermute | solution.py:820
  13.7 77.8 %collective-permute-start.22 = (bf16[64,512]{1,0:T(8,128)(2,1)}, bf16[64,512]{1,0:T(8,128)(2,1)}, u32[]{:S(2)}, u32[]{:S(2)}) collective-permute-start(bf16[64,512]{1,0:T(8,128)(2,1)} %pad_maximum_fusion.20), channel_id=1, source_target_pairs={{0,16},{8,24},{16,0},{24,8},{1,17},{9,25},{17,1},{25,9},{2,18},{10... | collective-permute-start | bytes 196616 | tf_op jit(solution)/shard_map/ppermute | solution.py:820
  40.8 19.5 %collective-permute-start.11 = (bf16[64,1664]{1,0:T(8,128)(2,1)S(1)}, bf16[64,1664]{1,0:T(8,128)(2,1)S(1)}, u32[]{:S(2)}, u32[]{:S(2)}) collective-permute-start(bf16[64,1664]{1,0:T(8,128)(2,1)S(1)} %copy-done.14), channel_id=1, source_target_pairs={{0,16},{8,24},{16,0},{24,8},{1,17},{9,25},{17,1},{25,9},{2,18},{10... | collective-permute-start | bytes 638984 | tf_op jit(solution)/shard_map/ppermute | solution.py:820
  41.7 18.6 %collective-permute-start.10 = (bf16[64,1664]{1,0:T(8,128)(2,1)S(1)}, bf16[64,1664]{1,0:T(8,128)(2,1)S(1)}, u32[]{:S(2)}, u32[]{:S(2)}) collective-permute-start(bf16[64,1664]{1,0:T(8,128)(2,1)S(1)} %copy-done.14), channel_id=1, source_target_pairs={{0,8},{8,0},{16,24},{24,16},{1,9},{9,1},{17,25},{25,17},{2,10},{10... | collective-permute-start | bytes 638984 | tf_op jit(solution)/shard_map/ppermute | solution.py:820
  46.8 50.4 %collective-permute-start.31 = (bf16[64,1024]{1,0:T(8,128)(2,1)S(1)}, bf16[64,1024]{1,0:T(8,128)(2,1)S(1)}, u32[]{:S(2)}, u32[]{:S(2)}) collective-permute-start(bf16[64,1024]{1,0:T(8,128)(2,1)S(1)} %pad_maximum_fusion.18), channel_id=1, source_target_pairs={{0,24},{8,16},{16,8},{24,0},{1,25},{9,17},{17,9},{25,1},{2,26},{10... | collective-permute-start | bytes 393224 | tf_op jit(solution)/shard_map/ppermute | solution.py:820
  60.4 18.8 %collective-permute-start.14 = (bf16[4,64,1664]{2,1,0:T(8,128)(2,1)S(1)}, bf16[4,64,1664]{2,1,0:T(8,128)(2,1)S(1)}, u32[]{:S(2)}, u32[]{:S(2)}) collective-permute-start(bf16[4,64,1664]{2,1,0:T(8,128)(2,1)S(1)} %pad_maximum_fusion), channel_id=1, source_target_pairs={{0,2},{2,0},{1,3},{3,1},{4,6},{6,4},{5,7},{7,5},{8,10},{10,8},{9,1... | collective-permute-start | bytes 2555912 | tf_op jit(solution)/shard_map/ppermute | solution.py:820
  62.0 20.0 %collective-permute-start.13 = (bf16[4,64,1664]{2,1,0:T(8,128)(2,1)S(1)}, bf16[4,64,1664]{2,1,0:T(8,128)(2,1)S(1)}, u32[]{:S(2)}, u32[]{:S(2)}) collective-permute-start(bf16[4,64,1664]{2,1,0:T(8,128)(2,1)S(1)} %pad_maximum_fusion), channel_id=1, source_target_pairs={{0,4},{4,0},{1,5},{5,1},{2,6},{6,2},{3,7},{7,3},{8,12},{12,8},{9,1... | collective-permute-start | bytes 2555912 | tf_op jit(solution)/shard_map/ppermute | solution.py:820
  91.5 69.5 %collective-permute-start.17 = (bf16[16,64,1664]{2,1,0:T(8,128)(2,1)S(1)}, bf16[16,64,1664]{2,1,0:T(8,128)(2,1)}, u32[]{:S(2)}, u32[]{:S(2)}) collective-permute-start(bf16[16,64,1664]{2,1,0:T(8,128)(2,1)S(1)} %constant_dynamic-update-slice_fusion.15.own_hbm.norm_own_hbm), channel_id=1, source_target_pairs={{0,1},{1,0},{2,3},{3,2},{4,5},{5,4},{6,7},{7,6},{8,9},{9,8},{10,11... | collective-permute-start | bytes 10223624 | tf_op jit(solution)/shard_map/ppermute | solution.py:820
  100.3 19.3 %collective-permute-start.33 = (bf16[4,64,1024]{2,1,0:T(8,128)(2,1)S(1)}, bf16[4,64,1024]{2,1,0:T(8,128)(2,1)S(1)}, u32[]{:S(2)}, u32[]{:S(2)}) collective-permute-start(bf16[4,64,1024]{2,1,0:T(8,128)(2,1)S(1)} %pad_maximum_fusion.3), channel_id=1, source_target_pairs={{0,2},{2,0},{1,3},{3,1},{4,6},{6,4},{5,7},{7,5},{8,10},{10,8},{9,1... | collective-permute-start | bytes 1572872 | tf_op jit(solution)/shard_map/ppermute | solution.py:820
  103.4 18.3 %collective-permute-start.32 = (bf16[4,64,1024]{2,1,0:T(8,128)(2,1)S(1)}, bf16[4,64,1024]{2,1,0:T(8,128)(2,1)S(1)}, u32[]{:S(2)}, u32[]{:S(2)}) collective-permute-start(bf16[4,64,1024]{2,1,0:T(8,128)(2,1)S(1)} %pad_maximum_fusion.3), channel_id=1, source_target_pairs={{0,4},{4,0},{1,5},{5,1},{2,6},{6,2},{3,7},{7,3},{8,12},{12,8},{9,1... | collective-permute-start | bytes 1572872 | tf_op jit(solution)/shard_map/ppermute | solution.py:820
  106.0 15.1 %collective-permute-start.7 = (bf16[2,64,512]{2,1,0:T(8,128)(2,1)S(1)}, bf16[2,64,512]{2,1,0:T(8,128)(2,1)S(1)}, u32[]{:S(2)}, u32[]{:S(2)}) collective-permute-start(bf16[2,64,512]{2,1,0:T(8,128)(2,1)S(1)} %slice.708), channel_id=1, source_target_pairs={{0,4},{4,0},{1,5},{5,1},{2,6},{6,2},{3,7},{7,3},{8,12},{12,8},{9,1... | collective-permute-start | bytes 393224 | tf_op jit(solution)/shard_map/ppermute | solution.py:820
  109.1 28.8 %collective-permute-start.1 = (bf16[256,512]{1,0:T(8,128)(2,1)S(1)}, bf16[256,512]{1,0:T(8,128)(2,1)S(1)}, u32[]{:S(2)}, u32[]{:S(2)}) collective-permute-start(bf16[256,512]{1,0:T(8,128)(2,1)S(1)} %pad_maximum_fusion.13), channel_id=1, source_target_pairs={{1,0},{2,1},{3,2},{5,4},{6,5},{7,6},{9,8},{10,9},{11,10},{13,12},{... | collective-permute-start | bytes 786440 | tf_op jit(solution)/shard_map/ppermute | solution.py:892
  119.6 18.9 %collective-permute-start.24 = (bf16[4,64,512]{2,1,0:T(8,128)(2,1)S(1)}, bf16[4,64,512]{2,1,0:T(8,128)(2,1)S(1)}, u32[]{:S(2)}, u32[]{:S(2)}) collective-permute-start(bf16[4,64,512]{2,1,0:T(8,128)(2,1)S(1)} %pad_maximum_fusion.15), channel_id=1, source_target_pairs={{0,4},{4,0},{1,5},{5,1},{2,6},{6,2},{3,7},{7,3},{8,12},{12,8},{9,1... | collective-permute-start | bytes 786440 | tf_op jit(solution)/shard_map/ppermute | solution.py:820
  137.9 74.9 %collective-permute-start.36 = (bf16[16,64,1024]{2,1,0:T(8,128)(2,1)}, bf16[16,64,1024]{2,1,0:T(8,128)(2,1)}, u32[]{:S(2)}, u32[]{:S(2)}) collective-permute-start(bf16[16,64,1024]{2,1,0:T(8,128)(2,1)} %constant_dynamic-update-slice_fusion.31.own_hbm), channel_id=1, source_target_pairs={{0,1},{1,0},{2,3},{3,2},{4,5},{5,4},{6,7},{7,6},{8,9},{9,8},{10,11... | collective-permute-start | bytes 6291464 | tf_op jit(solution)/shard_map/ppermute | solution.py:820
  148.0 50.6 %collective-permute-start.28 = (bf16[16,64,512]{2,1,0:T(8,128)(2,1)}, bf16[16,64,512]{2,1,0:T(8,128)(2,1)}, u32[]{:S(2)}, u32[]{:S(2)}) collective-permute-start(bf16[16,64,512]{2,1,0:T(8,128)(2,1)} %constant_dynamic-update-slice_fusion.23.own_hbm), channel_id=1, source_target_pairs={{0,1},{1,0},{2,3},{3,2},{4,5},{5,4},{6,7},{7,6},{8,9},{9,8},{10,11... | collective-permute-start | bytes 3145736 | tf_op jit(solution)/shard_map/ppermute | solution.py:820
  172.9 25.7 %collective-permute-start.18 = (bf16[384,512]{1,0:T(8,128)(2,1)}, bf16[384,512]{1,0:T(8,128)(2,1)S(1)}, u32[]{:S(2)}, u32[]{:S(2)}) collective-permute-start(bf16[384,512]{1,0:T(8,128)(2,1)} %get-tuple-element.54.m0_hbm), channel_id=1, source_target_pairs={{0,1},{1,0},{2,3},{3,2},{4,5},{5,4},{6,7},{7,6},{8,9},{9,8},{10,11... | collective-permute-start | bytes 1179656 | tf_op jit(solution)/shard_map/ppermute | solution.py:820
  182.3 16.3 %collective-permute-start.20 = (bf16[384,512]{1,0:T(8,128)(2,1)S(1)}, bf16[384,512]{1,0:T(8,128)(2,1)S(1)}, u32[]{:S(2)}, u32[]{:S(2)}) collective-permute-start(bf16[384,512]{1,0:T(8,128)(2,1)S(1)} %collective-permute-done.19.m2_hbm), channel_id=1, source_target_pairs={{0,1},{1,0},{2,3},{3,2},{4,5},{5,4},{6,7},{7,6},{8,9},{9,8},{10,11... | collective-permute-start | bytes 1179656 | tf_op jit(solution)/shard_map/ppermute | solution.py:820
  253.4 15.4 %collective-permute-start.38 = (bf16[384,512]{1,0:T(8,128)(2,1)S(1)}, bf16[384,512]{1,0:T(8,128)(2,1)S(1)}, u32[]{:S(2)}, u32[]{:S(2)}) collective-permute-start(bf16[384,512]{1,0:T(8,128)(2,1)S(1)} %fusion), channel_id=1, source_target_pairs={{0,2},{2,0},{1,3},{3,1},{4,6},{6,4},{5,7},{7,5},{8,10},{10,8},{9,1... | collective-permute-start | bytes 1179656 | tf_op jit(solution)/shard_map/ppermute | solution.py:820
  268.3 44.3 %collective-permute-start.49 = (bf16[16,64,1024]{2,1,0:T(8,128)(2,1)}, bf16[16,64,1024]{2,1,0:T(8,128)(2,1)}, u32[]{:S(2)}, u32[]{:S(2)}) collective-permute-start(bf16[16,64,1024]{2,1,0:T(8,128)(2,1)} %get-tuple-element.123), channel_id=1, source_target_pairs={{0,1},{1,0},{2,3},{3,2},{4,5},{5,4},{6,7},{7,6},{8,9},{9,8},{10,11... | collective-permute-start | bytes 6291464 | tf_op jit(solution)/shard_map/ppermute | solution.py:820
  268.5 57.6 %collective-permute-start.41 = (bf16[16,64,1024]{2,1,0:T(8,128)(2,1)}, bf16[16,64,1024]{2,1,0:T(8,128)(2,1)S(1)}, u32[]{:S(2)}, u32[]{:S(2)}) collective-permute-start(bf16[16,64,1024]{2,1,0:T(8,128)(2,1)} %get-tuple-element.121), channel_id=1, source_target_pairs={{0,1},{1,0},{2,3},{3,2},{4,5},{5,4},{6,7},{7,6},{8,9},{9,8},{10,11... | collective-permute-start | bytes 6291464 | tf_op jit(solution)/shard_map/ppermute | solution.py:820
  304.6 21.1 %collective-permute-start.65 = (bf16[16,64,512]{2,1,0:T(8,128)(2,1)}, bf16[16,64,512]{2,1,0:T(8,128)(2,1)S(1)}, u32[]{:S(2)}, u32[]{:S(2)}) collective-permute-start(bf16[16,64,512]{2,1,0:T(8,128)(2,1)} %get-tuple-element.127), channel_id=1, source_target_pairs={{0,1},{1,0},{2,3},{3,2},{4,5},{5,4},{6,7},{7,6},{8,9},{9,8},{10,11... | collective-permute-start | bytes 3145736 | tf_op jit(solution)/shard_map/ppermute | solution.py:820
  306.3 70.3 %collective-permute-start.57 = (bf16[16,64,1024]{2,1,0:T(8,128)(2,1)}, bf16[16,64,1024]{2,1,0:T(8,128)(2,1)S(1)}, u32[]{:S(2)}, u32[]{:S(2)}) collective-permute-start(bf16[16,64,1024]{2,1,0:T(8,128)(2,1)} %get-tuple-element.125), channel_id=1, source_target_pairs={{0,1},{1,0},{2,3},{3,2},{4,5},{5,4},{6,7},{7,6},{8,9},{9,8},{10,11... | collective-permute-start | bytes 6291464 | tf_op jit(solution)/shard_map/ppermute | solution.py:820
  314.3 20.4 %collective-permute-start.52 = (bf16[2,64,1024]{2,1,0:T(8,128)(2,1)S(1)}, bf16[2,64,1024]{2,1,0:T(8,128)(2,1)S(1)}, u32[]{:S(2)}, u32[]{:S(2)}) collective-permute-start(bf16[2,64,1024]{2,1,0:T(8,128)(2,1)S(1)} %get-tuple-element.172), channel_id=1, source_target_pairs={{0,4},{4,0},{1,5},{5,1},{2,6},{6,2},{3,7},{7,3},{8,12},{12,8},{9,1... | collective-permute-start | bytes 786440 | tf_op jit(solution)/shard_map/ppermute | solution.py:820
  321.7 14.9 %collective-permute-start.50 = (bf16[2,64,1024]{2,1,0:T(8,128)(2,1)S(1)}, bf16[2,64,1024]{2,1,0:T(8,128)(2,1)S(1)}, u32[]{:S(2)}, u32[]{:S(2)}) collective-permute-start(bf16[2,64,1024]{2,1,0:T(8,128)(2,1)S(1)} %get-tuple-element.173), channel_id=1, source_target_pairs={{0,2},{2,0},{1,3},{3,1},{4,6},{6,4},{5,7},{7,5},{8,10},{10,8},{9,1... | collective-permute-start | bytes 786440 | tf_op jit(solution)/shard_map/ppermute | solution.py:820
  340.8 19.6 %collective-permute-start.53 = (bf16[4,64,1024]{2,1,0:T(8,128)(2,1)S(1)}, bf16[4,64,1024]{2,1,0:T(8,128)(2,1)S(1)}, u32[]{:S(2)}, u32[]{:S(2)}) collective-permute-start(bf16[4,64,1024]{2,1,0:T(8,128)(2,1)S(1)} %pad_maximum_fusion.9), channel_id=1, source_target_pairs={{0,2},{2,0},{1,3},{3,1},{4,6},{6,4},{5,7},{7,5},{8,10},{10,8},{9,1... | collective-permute-start | bytes 1572872 | tf_op jit(solution)/shard_map/ppermute | solution.py:820
  353.6 14.9 %collective-permute-start.51 = (bf16[4,64,1024]{2,1,0:T(8,128)(2,1)S(1)}, bf16[4,64,1024]{2,1,0:T(8,128)(2,1)S(1)}, u32[]{:S(2)}, u32[]{:S(2)}) collective-permute-start(bf16[4,64,1024]{2,1,0:T(8,128)(2,1)S(1)} %pad_maximum_fusion.8), channel_id=1, source_target_pairs={{0,4},{4,0},{1,5},{5,1},{2,6},{6,2},{3,7},{7,3},{8,12},{12,8},{9,1... | collective-permute-start | bytes 1572872 | tf_op jit(solution)/shard_map/ppermute | solution.py:820
  355.6 15.1 %collective-permute-start.45 = (bf16[4,64,1024]{2,1,0:T(8,128)(2,1)S(1)}, bf16[4,64,1024]{2,1,0:T(8,128)(2,1)S(1)}, u32[]{:S(2)}, u32[]{:S(2)}) collective-permute-start(bf16[4,64,1024]{2,1,0:T(8,128)(2,1)S(1)} %pad_maximum_fusion.7), channel_id=1, source_target_pairs={{0,2},{2,0},{1,3},{3,1},{4,6},{6,4},{5,7},{7,5},{8,10},{10,8},{9,1... | collective-permute-start | bytes 1572872 | tf_op jit(solution)/shard_map/ppermute | solution.py:820
  357.1 17.4 %collective-permute-start.43 = (bf16[4,64,1024]{2,1,0:T(8,128)(2,1)S(1)}, bf16[4,64,1024]{2,1,0:T(8,128)(2,1)S(1)}, u32[]{:S(2)}, u32[]{:S(2)}) collective-permute-start(bf16[4,64,1024]{2,1,0:T(8,128)(2,1)S(1)} %pad_maximum_fusion.6), channel_id=1, source_target_pairs={{0,4},{4,0},{1,5},{5,1},{2,6},{6,2},{3,7},{7,3},{8,12},{12,8},{9,1... | collective-permute-start | bytes 1572872 | tf_op jit(solution)/shard_map/ppermute | solution.py:820
  370.6 17.7 %collective-permute-start.55 = (bf16[64,1024]{1,0:T(8,128)(2,1)S(1)}, bf16[64,1024]{1,0:T(8,128)(2,1)S(1)}, u32[]{:S(2)}, u32[]{:S(2)}) collective-permute-start(bf16[64,1024]{1,0:T(8,128)(2,1)S(1)} %get-tuple-element.160), channel_id=1, source_target_pairs={{0,16},{8,24},{16,0},{24,8},{1,17},{9,25},{17,1},{25,9},{2,18},{10... | collective-permute-start | bytes 393224 | tf_op jit(solution)/shard_map/ppermute | solution.py:820
  (96 other events, 1063.4 us)
